TPU v7x, 32 devices: a whole 2x2x4 slice. The times are simulated.
32 devices in a mesh: dp: 4 (over x, core), row: 2 (over y), col: 4 (over z).
Axes of the slice: x: 2, y: 2, z: 4, core: 2. Of those that a mesh axis runs over, the one named last changes fastest.
Arguments:
- layer_input: bfloat16 [4096, 1024], P(('dp', 'col'), 'row'), may hold values from -6 to 6
- lengths: int32 [8], P('dp'), may hold values from 1 to 512, as said below
- attend_weight: bfloat16 [1024, 3072], P('row', 'col'), may hold values from -0.1875 to 0.1875
- attend_bias: float32 [16, 128], P('col'), may hold values from -0.6 to 0.6
- mixer_weight: bfloat16 [1024, 1024], P('col', 'row'), may hold values from -1.5 to 1.5
- mixer_bias: float32 [1024], P('row'), may hold values from -3 to 3
- first_gain: float32 [1024], P('row'), may hold values from 0.1 to 1.9
- first_shift: float32 [1024], P('row'), may hold values from -3 to 3
- widen_weight: bfloat16 [1024, 4096], P('row', 'col'), may hold values from -0.1875 to 0.1875
- widen_bias: float32 [4096], P('col'), may hold values from -3 to 3
- narrow_weight: bfloat16 [4096, 1024], P('col', 'row'), may hold values from -0.09375 to 0.09375
- narrow_bias: float32 [1024], P('row'), may hold values from -3 to 3
- second_gain: float32 [1024], P('row'), may hold values from 0.1 to 1.9
- second_shift: float32 [1024], P('row'), may hold values from -3 to 3
- cotangent: bfloat16 [4096, 1024], P(('dp', 'col'), 'row'), may hold values from -6 to 6
Outputs:
- layer_output: bfloat16 [4096, 1024], P(('dp', 'col'), 'row')
- input_gradient: float32 [4096, 1024], P(('dp', 'col'), 'row')
- attend_weight_gradient: float32 [1024, 3072], P('row', 'col')
- attend_bias_gradient: float32 [16, 128], P('col')
- mixer_weight_gradient: float32 [1024, 1024], P('col', 'row')
- mixer_bias_gradient: float32 [1024], P('row')
- first_gain_gradient: float32 [1024], P('row')
- first_shift_gradient: float32 [1024], P('row')
- widen_weight_gradient: float32 [1024, 4096], P('row', 'col')
- widen_bias_gradient: float32 [4096], P('col')
- narrow_weight_gradient: float32 [4096, 1024], P('col', 'row')
- narrow_bias_gradient: float32 [1024], P('row')
- second_gain_gradient: float32 [1024], P('row')
- second_shift_gradient: float32 [1024], P('row')
Inputs may be any that keep to these rules, and one draw needn't show every extreme that they name: lengths[s] is the length of the sequence in slot s; a replica's 2 slots are consecutive entries; some slot holds the full 512 rows.
All inputs are finite; a program needn't handle non-finite values.
Results may differ from a plain program's by a relative error of at most 0.015.
Values may be sent and summed in bfloat16 or wider, within the bound.
A program may use at most 128 MiB of HBM per device.

v0:
```python
import jax
import jax.numpy as jnp
from jax import lax
from jax.sharding import PartitionSpec as P

D = 1024
HD = 64


EPSILON = 1e-12
MASKED = -1e30


def product(left_side, right_side):
    return jnp.dot(left_side, right_side, preferred_element_type=jnp.float32)


def inner_rows(left_side, right_side):
    return lax.dot_general(
        left_side, right_side, (((0,), (0,)), ((), ())), preferred_element_type=jnp.float32
    )


def outer_back(left_side, right_side):
    return lax.dot_general(
        left_side, right_side, (((1,), (1,)), ((), ())), preferred_element_type=jnp.float32
    )


def gelu_exact(values):
    return jax.nn.gelu(values, approximate=False)


def gather_tokens(local_block):
    return lax.all_gather(local_block, "col", axis=0, tiled=True)


def sum_tokens(left_side, right_side, multiply):
    return lax.psum_scatter(multiply(left_side, right_side), "col", scatter_dimension=0, tiled=True)


def scatter_units(partial_value):
    return lax.psum_scatter(partial_value, "row", scatter_dimension=1, tiled=True)


def gather_units(local_block):
    return lax.all_gather(local_block, "row", axis=1, tiled=True)


def norm_sums(first_sum, second_sum):
    return lax.psum((first_sum, second_sum), "row")


def norm_forward(summed, gain_row, shift_row):
    row_total, squares = norm_sums(
        jnp.sum(summed, axis=1, keepdims=True), jnp.sum(summed * summed, axis=1, keepdims=True)
    )
    average = row_total / D
    variance = squares / D - average * average
    inverse = lax.rsqrt(variance + EPSILON)
    normal = (summed - average) * inverse
    return (normal * gain_row + shift_row, normal, inverse)


def norm_backward(upstream, normal, inverse, gain_row):
    scaled = upstream * gain_row
    row_total, crossed = norm_sums(
        jnp.sum(scaled, axis=1, keepdims=True), jnp.sum(scaled * normal, axis=1, keepdims=True)
    )
    return (scaled - row_total / D - normal * (crossed / D)) * inverse


def slot_scores(query_part, key_part, length):
    scores = jnp.einsum(
        "qhd,khd->hqk", query_part, key_part, preferred_element_type=jnp.float32
    ) * HD ** (-0.5)
    valid_keys = lax.iota(jnp.int32, key_part.shape[0]) < length
    return jnp.where(valid_keys[None, None, :], scores, MASKED)


def slot_forward(slot_item):
    query_part, key_part, value_part, length = slot_item
    scores = slot_scores(query_part, key_part, length)
    row_top = jnp.max(scores, axis=2, keepdims=True)
    exponent = jnp.exp(scores - row_top)
    row_total = jnp.sum(exponent, axis=2, keepdims=True)
    probabilities = (exponent / row_total).astype(jnp.bfloat16)
    mixed = jnp.einsum(
        "hqk,khd->qhd", probabilities, value_part, preferred_element_type=jnp.float32
    )
    return (mixed.astype(jnp.bfloat16), (row_top + jnp.log(row_total))[:, :, 0])


def slot_backward(slot_item):
    query_part, key_part, value_part, length, logsum, grad_heads = slot_item
    probabilities = jnp.exp(slot_scores(query_part, key_part, length) - logsum[:, :, None])
    grad_probs = jnp.einsum(
        "qhd,khd->hqk", grad_heads, value_part, preferred_element_type=jnp.float32
    )
    grad_values = jnp.einsum(
        "hqk,qhd->khd",
        probabilities.astype(jnp.bfloat16),
        grad_heads,
        preferred_element_type=jnp.float32,
    )
    along = jnp.sum(probabilities * grad_probs, axis=2, keepdims=True)
    grad_scores = (probabilities * (grad_probs - along)).astype(jnp.bfloat16)
    grad_query = jnp.einsum(
        "hqk,khd->qhd", grad_scores, key_part, preferred_element_type=jnp.float32
    ) * HD ** (-0.5)
    grad_keys = jnp.einsum(
        "hqk,qhd->khd", grad_scores, query_part, preferred_element_type=jnp.float32
    ) * HD ** (-0.5)
    return jnp.stack([grad_query, grad_keys, grad_values], axis=2)


def per_device(
    layer_input,
    lengths,
    attend_weight,
    attend_bias,
    mixer_weight,
    mixer_bias,
    first_gain,
    first_shift,
    widen_weight,
    widen_bias,
    narrow_weight,
    narrow_bias,
    second_gain,
    second_shift,
    cotangent,
):
    row_rank = lax.axis_index("row")
    col_rank = lax.axis_index("col")
    row_count = lax.axis_size("row")
    col_count = lax.axis_size("col")
    local_rows = layer_input.shape[0]
    replica_rows = local_rows * col_count
    slot_count = lengths.shape[0]
    seq_len = replica_rows // slot_count
    heads_here = attend_bias.shape[0] // row_count
    units_here = widen_bias.shape[0] // row_count
    gathered_input = gather_tokens(layer_input)
    packed = scatter_units(product(gathered_input, attend_weight))
    bias_here = lax.dynamic_slice_in_dim(attend_bias, row_rank * heads_here, heads_here, 0)
    bias_full = jnp.concatenate(
        [bias_here[:, :HD], jnp.zeros((heads_here, HD), jnp.float32), bias_here[:, HD:]], axis=1
    ).reshape(heads_here * 3 * HD)
    packed = (packed + bias_full).astype(jnp.bfloat16)
    split_heads = packed.reshape(slot_count, seq_len, heads_here, 3, HD)
    query_all = split_heads[:, :, :, 0]
    keys_all = split_heads[:, :, :, 1]
    values_all = split_heads[:, :, :, 2]
    mixed, logsum = lax.map(slot_forward, (query_all, keys_all, values_all, lengths))
    mixed_rows = mixed.reshape(replica_rows, heads_here * HD)
    mixed_block = gather_units(mixed_rows)
    attended = sum_tokens(mixed_block, mixer_weight, product)
    attended = attended + mixer_bias
    first_out, first_normal, first_inverse = norm_forward(
        layer_input.astype(jnp.float32) + attended, first_gain, first_shift
    )
    gathered_first = gather_tokens(first_out.astype(jnp.bfloat16))
    widened = scatter_units(product(gathered_first, widen_weight))
    widened = widened + lax.dynamic_slice_in_dim(widen_bias, row_rank * units_here, units_here, 0)
    active, gelu_pull = jax.vjp(gelu_exact, widened)
    active_block = gather_units(active.astype(jnp.bfloat16))
    narrowed = sum_tokens(active_block, narrow_weight, product) + narrow_bias
    second_out, second_normal, second_inverse = norm_forward(
        first_out + narrowed, second_gain, second_shift
    )
    layer_output = second_out.astype(jnp.bfloat16)
    positions = col_rank * local_rows + lax.iota(jnp.int32, local_rows)
    slot_of = positions // seq_len
    length_of = jnp.sum(
        jnp.where(
            slot_of[:, None] == lax.iota(jnp.int32, slot_count)[None, :], lengths[None, :], 0
        ),
        axis=1,
    )
    upstream = jnp.where(
        (positions % seq_len < length_of)[:, None], cotangent.astype(jnp.float32), 0.0
    )
    second_gain_part = jnp.sum(upstream * second_normal, axis=0)
    second_shift_part = jnp.sum(upstream, axis=0)
    grad_second = norm_backward(upstream, second_normal, second_inverse, second_gain)
    grad_narrowed = grad_second.astype(jnp.bfloat16)
    narrow_bias_part = jnp.sum(grad_narrowed, axis=0, dtype=jnp.float32)
    grad_narrow_block = gather_tokens(grad_narrowed)
    narrow_weight_part = inner_rows(active_block, grad_narrow_block)
    grad_active = scatter_units(outer_back(grad_narrow_block, narrow_weight))
    grad_widened = gelu_pull(grad_active)[0].astype(jnp.bfloat16)
    widen_bias_part = jnp.sum(grad_widened, axis=0, dtype=jnp.float32)
    grad_widen_block = gather_units(grad_widened)
    widen_weight_part = inner_rows(gathered_first, grad_widen_block)
    grad_first = sum_tokens(grad_widen_block, widen_weight, outer_back) + grad_second
    first_gain_part = jnp.sum(grad_first * first_normal, axis=0)
    first_shift_part = jnp.sum(grad_first, axis=0)
    grad_attended = norm_backward(grad_first, first_normal, first_inverse, first_gain)
    grad_mix = grad_attended.astype(jnp.bfloat16)
    mixer_bias_part = jnp.sum(grad_mix, axis=0, dtype=jnp.float32)
    grad_mixer_block = gather_tokens(grad_mix)
    mixer_weight_part = inner_rows(mixed_block, grad_mixer_block)
    grad_mixed = scatter_units(outer_back(grad_mixer_block, mixer_weight)).astype(jnp.bfloat16)
    grad_heads = grad_mixed.reshape(slot_count, seq_len, heads_here, HD)
    grad_slots = lax.map(
        slot_backward, (query_all, keys_all, values_all, lengths, logsum, grad_heads)
    )
    grad_packed = grad_slots.reshape(replica_rows, heads_here * 3 * HD).astype(jnp.bfloat16)
    packed_sums = jnp.sum(grad_packed, axis=0, dtype=jnp.float32).reshape(heads_here, 3, HD)
    attend_bias_part = jnp.concatenate([packed_sums[:, 0], packed_sums[:, 2]], axis=1)
    grad_attend_block = gather_units(grad_packed)
    attend_weight_part = inner_rows(gathered_input, grad_attend_block)
    input_gradient = sum_tokens(grad_attend_block, attend_weight, outer_back) + grad_attended
    weight_totals = (
        lax.psum(attend_weight_part.astype(jnp.bfloat16), "dp").astype(jnp.float32),
        lax.psum(mixer_weight_part.astype(jnp.bfloat16), "dp").astype(jnp.float32),
        lax.psum(widen_weight_part.astype(jnp.bfloat16), "dp").astype(jnp.float32),
        lax.psum(narrow_weight_part.astype(jnp.bfloat16), "dp").astype(jnp.float32),
    )
    selector = lax.iota(jnp.int32, row_count) == row_rank
    attend_padded = jnp.where(selector[:, None, None], attend_bias_part[None], 0.0).reshape(
        row_count * heads_here, 2 * HD
    )
    widen_padded = jnp.where(selector[:, None], widen_bias_part[None], 0.0).reshape(
        row_count * units_here
    )
    column_totals = lax.psum((attend_padded, widen_padded), ("dp", "row"))
    vector_totals = lax.psum(
        (
            mixer_bias_part,
            first_gain_part,
            first_shift_part,
            narrow_bias_part,
            second_gain_part,
            second_shift_part,
        ),
        ("dp", "col"),
    )
    return (
        layer_output,
        input_gradient,
        weight_totals[0],
        column_totals[0],
        weight_totals[1],
        vector_totals[0],
        vector_totals[1],
        vector_totals[2],
        weight_totals[2],
        column_totals[1],
        weight_totals[3],
        vector_totals[3],
        vector_totals[4],
        vector_totals[5],
    )


def solution(mesh):
    return jax.shard_map(
        per_device,
        mesh=mesh,
        in_specs=(
            P(("dp", "col"), "row"),
            P("dp"),
            P("row", "col"),
            P("col", None),
            P("col", "row"),
            P("row"),
            P("row"),
            P("row"),
            P("row", "col"),
            P("col"),
            P("col", "row"),
            P("row"),
            P("row"),
            P("row"),
            P(("dp", "col"), "row"),
        ),
        out_specs=(
            P(("dp", "col"), "row"),
            P(("dp", "col"), "row"),
            P("row", "col"),
            P("col", None),
            P("col", "row"),
            P("row"),
            P("row"),
            P("row"),
            P("row", "col"),
            P("col"),
            P("col", "row"),
            P("row"),
            P("row"),
            P("row"),
        ),
        check_vma=False,
    )
```

profile of v0, /device:TPU:8, one launch (start us, length us, event | category | flops | bytes accessed | tf_op | source)
XLA Modules:
  0.0 742.0 jit_solution(12799276565684024016)
XLA Ops:
  8.0 30.7 %all-gather.8.cloned.1.call-done = bf16[1024,512]{1,0:T(8,128)(2,1)} async-done(((bf16[256,512]{1,0:T(8,128)(2,1)}), bf16[1024,512]{1,0:T(8,128)(2,1)}) %all-gather.8.cloned.1.call-update) | async-done | bytes 1048592 | tf_op jit(solution)/shard_map/all_gather | solution.py:35
  38.7 4.1 fusion.61
  43.6 42.2 %reduce-scatter.9.cloned.1.call-done = f32[1024,384]{1,0:T(8,128)} async-done(((f32[1024,768]{1,0:T(8,128)}), f32[1024,384]{1,0:T(8,128)}) %reduce-scatter.9.cloned.1.call-update) | async-done | bytes 1572880 | tf_op jit(solution)/shard_map/reduce_scatter | solution.py:43
  88.9 6.1 while.22
  95.3 8.7 %all_gather.25 = bf16[1024,256]{0,1:T(8,128)(2,1)S(1)} all-gather(bf16[1024,128]{0,1:T(8,128)(2,1)S(1)} %bitcast.177), channel_id=1, replica_groups=mesh['dp'=4,'row'=2,'col'=4] {'row'}, dimensions={1}, use_global_device_ids=true | all-gather | bytes 786432 | tf_op jit(solution)/shard_map/all_gather | solution.py:47
  105.9 41.7 %reduce-scatter.11.cloned.1.call-done = f32[256,512]{1,0:T(8,128)} async-done(((f32[1024,512]{1,0:T(8,128)}), f32[256,512]{1,0:T(8,128)}) %reduce-scatter.11.cloned.1.call-update) | async-done | bytes 524304 | tf_op jit(solution)/shard_map/reduce_scatter | solution.py:39
  148.9 4.9 all-reduce.5
  154.8 29.6 %all-gather.10.cloned.1.call-done = bf16[1024,512]{1,0:T(8,128)(2,1)} async-done(((bf16[256,512]{1,0:T(8,128)(2,1)}), bf16[1024,512]{1,0:T(8,128)(2,1)}) %all-gather.10.cloned.1.call-update) | async-done | bytes 1048592 | tf_op jit(solution)/shard_map/all_gather | solution.py:35
  184.4 4.7 fusion.63
  189.9 53.3 %reduce-scatter.13.cloned.1.call-done = f32[1024,512]{1,0:T(8,128)} async-done(((f32[1024,1024]{1,0:T(8,128)}), f32[1024,512]{1,0:T(8,128)}) %reduce-scatter.13.cloned.1.call-update) | async-done | bytes 2097168 | tf_op jit(solution)/shard_map/reduce_scatter | solution.py:43
  243.1 6.7 multiply_convert_fusion.1
  249.9 33.2 %all-gather.12.cloned.1.call-done = bf16[1024,1024]{1,0:T(8,128)(2,1)} async-done(((bf16[1024,512]{1,0:T(8,128)(2,1)}), bf16[1024,1024]{1,0:T(8,128)(2,1)}) %all-gather.12.cloned.1.call-update) | async-done | bytes 2097168 | tf_op jit(solution)/shard_map/all_gather | solution.py:47
  283.1 4.2 fusion.64
  287.5 41.6 %reduce-scatter.15.cloned.1.call-done = f32[256,512]{1,0:T(8,128)} async-done(((f32[1024,512]{1,0:T(8,128)}), f32[256,512]{1,0:T(8,128)}) %reduce-scatter.15.cloned.1.call-update) | async-done | bytes 524304 | tf_op jit(solution)/shard_map/reduce_scatter | solution.py:39
  330.4 4.9 all-reduce.4
  336.7 4.9 all-reduce.3
  343.6 29.6 %all-gather.14.cloned.1.call-done = bf16[1024,512]{1,0:T(8,128)(2,1)} async-done(((bf16[256,512]{1,0:T(8,128)(2,1)}), bf16[1024,512]{1,0:T(8,128)(2,1)}) %all-gather.14.cloned.1.call-update) | async-done | bytes 1048592 | tf_op jit(solution)/shard_map/all_gather | solution.py:35
  373.2 4.4 fusion.65
  377.9 53.7 %reduce-scatter.17.cloned.1.call-done = f32[1024,512]{1,0:T(8,128)} async-done(((f32[1024,1024]{1,0:T(8,128)}), f32[1024,512]{1,0:T(8,128)}) %reduce-scatter.17.cloned.1.call-update) | async-done | bytes 2097168 | tf_op jit(solution)/shard_map/reduce_scatter | solution.py:43
  431.7 4.9 convert_reduce_fusion
  436.6 33.2 %all-gather.16.cloned.1.call-done = bf16[1024,1024]{1,0:T(8,128)(2,1)} async-done(((bf16[1024,512]{1,0:T(8,128)(2,1)}), bf16[1024,1024]{1,0:T(8,128)(2,1)}) %all-gather.16.cloned.1.call-update) | async-done | bytes 2097168 | tf_op jit(solution)/shard_map/all_gather | solution.py:47
  469.9 4.2 fusion.66
  474.2 41.7 %reduce-scatter.19.cloned.1.call-done = f32[256,512]{1,0:T(8,128)} async-done(((f32[1024,512]{1,0:T(8,128)}), f32[256,512]{1,0:T(8,128)}) %reduce-scatter.19.cloned.1.call-update) | async-done | bytes 524304 | tf_op jit(solution)/shard_map/reduce_scatter | solution.py:39
  518.1 4.9 all-reduce.2
  524.2 29.6 %all-gather.18.cloned.1.call-done = bf16[1024,512]{1,0:T(8,128)(2,1)} async-done(((bf16[256,512]{1,0:T(8,128)(2,1)}), bf16[1024,512]{1,0:T(8,128)(2,1)}) %all-gather.18.cloned.1.call-update) | async-done | bytes 1048592 | tf_op jit(solution)/shard_map/all_gather | solution.py:35
  556.5 19.9 %reduce-scatter.21.cloned.1.call-done = f32[1024,128]{1,0:T(8,128)} async-done(((f32[1024,256]{1,0:T(8,128)}), f32[1024,128]{1,0:T(8,128)}) %reduce-scatter.21.cloned.1.call-update) | async-done | bytes 524304 | tf_op jit(solution)/shard_map/reduce_scatter | solution.py:43
  578.2 8.8 %while.23 = (s32[]{:T(128)}, bf16[2,512,2,3,64]{1,4,2,3,0:T(8,128)(2,1)S(1)}, bf16[2,512,2,64]{1,3,2,0:T(8,128)(2,1)S(1)}, s32[2]{0:T(128)S(1)}, bf16[2,512,2,64...) while((s32[]{:T(128)}, ...), condition=%wide.region_30.31_spmd, body=%wide.region_28.30_spmd.sunk | while | flops 341704192 | bytes 17849480 | solution.py:206
  588.9 4.3 convolution_convert_fusion.1
  596.6 19.6 %all-gather.20.cloned.1.call-done = bf16[1024,768]{0,1:T(8,128)(2,1)} async-done(((bf16[1024,384]{0,1:T(8,128)(2,1)}), bf16[1024,768]{0,1:T(8,128)(2,1)}) %all-gather.20.cloned.1.call-update) | async-done | bytes 1572880 | tf_op jit(solution)/shard_map/all_gather | solution.py:47
  623.8 59.1 %all-reduce = (f32[512]{0:T(512)}, f32[512]{0:T(512)}, f32[512]{0:T(512)}, f32[512]{0:T(512)}, f32[512]{0:T(512)}, /*index=5*/f32[512]{0:T(512)}) all-reduce(f32[512]{0:T(512)S(1)} %get-tuple-element.241, f32[512]{0:T(512)S(1)} %get-tuple-element.177, ...), channel_id=1, replica_groups=mesh['dp'=4,'row'=2,'col'=4] {'dp','col'}, use_global_device_ids=true, to_apply=%region_37.38 | all-reduce | flops 3072 | bytes 24576 | tf_op jit(solution)/shard_map/psum | solution.py:229
  683.2 13.4 %all-reduce.1 = (f32[4,128]{1,0:T(4,128)}, f32[1024]{0:T(1024)}) all-reduce(f32[4,128]{1,0:T(4,128)S(1)} %broadcast_select_fusion, f32[1024]{0:T(1024)S(1)} %bitcast.193), channel_id=1, replica_groups=mesh['dp'=4,'row'=2,'col'=4] {'dp','row'}, use_global_device_ids=true, to_apply=%region_34.35 | all-reduce | flops 1536 | bytes 12288 | tf_op jit(solution)/shard_map/psum | solution.py:228
  704.3 29.3 %reduce-scatter.23.cloned.1.call-done = f32[256,512]{1,0:T(8,128)} async-done(((f32[1024,512]{1,0:T(8,128)}), f32[256,512]{1,0:T(8,128)}) %reduce-scatter.23.cloned.1.call-update) | async-done | bytes 524304 | tf_op jit(solution)/shard_map/reduce_scatter | solution.py:39
  (179 shorter events, 60.2 us)
Async XLA Ops:
  7.2 275.9 %copy-start = (bf16[1024,512]{1,0:T(8,128)(2,1)S(1)}, bf16[1024,512]{1,0:T(8,128)(2,1)}, u32[]{:S(2)}) copy-start(bf16[1024,512]{1,0:T(8,128)(2,1)} %param.29) | copy-start | bytes 3145732
  7.2 31.5 %all-gather.8.cloned.1.call-start = ((), (), s32[]{:S(2)}) async-start(), calls=%async_computation.8 | async-start | bytes 1310720 | tf_op jit(solution)/shard_map/all_gather | solution.py:35
  7.9 77.9 %reduce-scatter.9.cloned.1.call-start = ((), (), s32[]{:S(2)}) async-start(), calls=%async_computation.9 | async-start | bytes 4718592 | tf_op jit(solution)/shard_map/reduce_scatter | solution.py:43
  42.8 104.8 %reduce-scatter.11.cloned.1.call-start = ((), (), s32[]{:S(2)}) async-start(), calls=%async_computation.10 | async-start | bytes 2621440 | tf_op jit(solution)/shard_map/reduce_scatter | solution.py:39
  88.9 15.2 %copy-start.13 = (bf16[256,512]{1,0:T(8,128)(2,1)S(1)}, bf16[256,512]{1,0:T(8,128)(2,1)}, u32[]{:S(2)}) copy-start(bf16[256,512]{1,0:T(8,128)(2,1)} %param.23) | copy-start | bytes 786436
  104.1 43.6 %copy-start.11 = (bf16[256,512]{1,0:T(8,128)(2,1)S(1)}, bf16[256,512]{1,0:T(8,128)(2,1)}, u32[]{:S(2)}) copy-start(bf16[256,512]{1,0:T(8,128)(2,1)} %param.19) | copy-start | bytes 786436
  104.1 43.6 %copy-start.19 = (f32[512]{0:T(512)S(1)}, f32[512]{0:T(512)}, u32[]{:S(2)}) copy-start(f32[512]{0:T(512)} %param.24) | copy-start | bytes 6148
  105.9 48.0 %copy-start.16 = (f32[512]{0:T(512)S(1)}, f32[512]{0:T(512)}, u32[]{:S(2)}) copy-start(f32[512]{0:T(512)} %param.25) | copy-start | bytes 6148
  105.9 48.0 %copy-start.18 = (f32[512]{0:T(512)S(1)}, f32[512]{0:T(512)}, u32[]{:S(2)}) copy-start(f32[512]{0:T(512)} %param.26) | copy-start | bytes 6148
  105.9 78.5 %all-gather.10.cloned.1.call-start = ((), (), s32[]{:S(2)}) async-start(), calls=%async_computation.11 | async-start | bytes 1310720 | tf_op jit(solution)/shard_map/all_gather | solution.py:35
  154.7 88.4 %reduce-scatter.13.cloned.1.call-start = ((), (), s32[]{:S(2)}) async-start(), calls=%async_computation.12 | async-start | bytes 6291456 | tf_op jit(solution)/shard_map/reduce_scatter | solution.py:43
  189.1 94.0 %all-gather.12.cloned.1.call-start = ((), (), s32[]{:S(2)}) async-start(), calls=%async_computation.13 | async-start | bytes 3145728 | tf_op jit(solution)/shard_map/all_gather | solution.py:47
  249.9 79.2 %reduce-scatter.15.cloned.1.call-start = ((), (), s32[]{:S(2)}) async-start(), calls=%async_computation.14 | async-start | bytes 2621440 | tf_op jit(solution)/shard_map/reduce_scatter | solution.py:39
  287.3 41.8 %copy-start.20 = (f32[512]{0:T(512)S(1)}, f32[512]{0:T(512)}, u32[]{:S(2)}) copy-start(f32[512]{0:T(512)} %param.30) | copy-start | bytes 6148
  287.3 48.1 %copy-start.17 = (f32[512]{0:T(512)S(1)}, f32[512]{0:T(512)}, u32[]{:S(2)}) copy-start(f32[512]{0:T(512)} %param.31) | copy-start | bytes 6148
  287.3 85.9 %all-gather.14.cloned.1.call-start = ((), (), s32[]{:S(2)}) async-start(), calls=%async_computation.15 | async-start | bytes 1310720 | tf_op jit(solution)/shard_map/all_gather | solution.py:35
  343.6 88.1 %reduce-scatter.17.cloned.1.call-start = ((), (), s32[]{:S(2)}) async-start(), calls=%async_computation.16 | async-start | bytes 6291456 | tf_op jit(solution)/shard_map/reduce_scatter | solution.py:43
  377.7 92.2 %all-gather.16.cloned.1.call-start = ((), (), s32[]{:S(2)}) async-start(), calls=%async_computation.17 | async-start | bytes 3145728 | tf_op jit(solution)/shard_map/all_gather | solution.py:47
  431.7 38.2 %copy-start.26 = (bf16[512,1024]{1,0:T(8,128)(2,1)S(1)}, bf16[512,1024]{1,0:T(8,128)(2,1)}, u32[]{:S(2)}) copy-start(bf16[512,1024]{1,0:T(8,128)(2,1)} %param.27) | copy-start | bytes 3145732
  436.6 79.3 %reduce-scatter.19.cloned.1.call-start = ((), (), s32[]{:S(2)}) async-start(), calls=%async_computation.18 | async-start | bytes 2621440 | tf_op jit(solution)/shard_map/reduce_scatter | solution.py:39
  474.1 41.8 %copy-start.6 = (bf16[256,512]{1,0:T(8,128)(2,1)S(1)}, bf16[256,512]{1,0:T(8,128)(2,1)}, u32[]{:S(2)}) copy-start(bf16[256,512]{1,0:T(8,128)(2,1)} %param.33) | copy-start | bytes 786436
  474.1 41.8 %copy-start.21 = (f32[512]{0:T(512)S(1)}, f32[512]{0:T(512)}, u32[]{:S(2)}) copy-start(f32[512]{0:T(512)} %param.32) | copy-start | bytes 6148
  474.1 79.7 %copy-start.14 = (bf16[256,512]{1,0:T(8,128)(2,1)S(1)}, bf16[256,512]{1,0:T(8,128)(2,1)}, u32[]{:S(2)}) copy-start(bf16[256,512]{1,0:T(8,128)(2,1)} %param.23) | copy-start | bytes 786436
  474.1 79.7 %all-gather.18.cloned.1.call-start = ((), (), s32[]{:S(2)}) async-start(), calls=%async_computation.19 | async-start | bytes 1310720 | tf_op jit(solution)/shard_map/all_gather | solution.py:35
  524.1 52.3 %reduce-scatter.21.cloned.1.call-start = ((), (), s32[]{:S(2)}) async-start(), calls=%async_computation.20 | async-start | bytes 1572864 | tf_op jit(solution)/shard_map/reduce_scatter | solution.py:43
  556.5 59.7 %all-gather.20.cloned.1.call-start = ((), (), s32[]{:S(2)}) async-start(), calls=%async_computation.21 | async-start | bytes 2359296 | tf_op jit(solution)/shard_map/all_gather | solution.py:47
  588.8 107.8 %all-reduce.9.cloned.1.call-start = ((), (), s32[]{:S(2)}) async-start(), calls=%async_computation.23 | async-start | bytes 6291456 | tf_op jit(solution)/shard_map/psum | solution.py:216
  593.2 23.0 %copy-start.3 = (bf16[1024,512]{1,0:T(8,128)(2,1)S(1)}, bf16[1024,512]{1,0:T(8,128)(2,1)}, u32[]{:S(2)}) copy-start(bf16[1024,512]{1,0:T(8,128)(2,1)} %all-gather.8.cloned.1.call-done) | copy-start | bytes 3145732
  619.5 114.1 %reduce-scatter.23.cloned.1.call-start = ((), (), s32[]{:S(2)}) async-start(), calls=%async_computation.22 | async-start | bytes 2621440 | tf_op jit(solution)/shard_map/reduce_scatter | solution.py:39
  623.5 59.4 %copy-start.5 = (bf16[2,512,2,3,64]{1,4,2,3,0:T(8,128)(2,1)S(1)}, bf16[2,512,2,3,64]{1,4,2,3,0:T(8,128)(2,1)}, u32[]{:S(2)}) copy-start(bf16[2,512,2,3,64]{1,4,2,3,0:T(8,128)(2,1)} %copy-done.4) | copy-start | bytes 2359300
  702.7 30.9 %copy-start.7 = (f32[256,512]{1,0:T(8,128)S(1)}, f32[256,512]{1,0:T(8,128)}, u32[]{:S(2)}) copy-start(f32[256,512]{1,0:T(8,128)} %get-tuple-element.243) | copy-start | bytes 1572868
  702.7 32.8 %copy-start.1 = (bf16[1024,512]{1,0:T(8,128)(2,1)S(1)}, bf16[1024,512]{1,0:T(8,128)(2,1)}, u32[]{:S(2)}) copy-start(bf16[1024,512]{1,0:T(8,128)(2,1)} %param.29) | copy-start | bytes 3145732
  (11 other events, 24.2 us)
Sparse Core Ops, SparseCore 0:
  9.6 29.0 all-gather.7
  42.9 42.8 reduce-scatter.8
  106.0 41.5 reduce-scatter.10
  154.9 29.4 all-gather.9
  189.3 53.8 reduce-scatter.12
  250.0 33.0 all-gather.11
  287.4 41.5 reduce-scatter.14
  343.7 29.4 all-gather.13
  377.8 53.8 reduce-scatter.16
  436.7 33.1 all-gather.15
  474.2 41.5 reduce-scatter.18
  524.2 29.4 all-gather.17
  556.6 19.8 reduce-scatter.20
  588.9 27.2 all-gather.19
  620.0 69.3 all-reduce.8
  691.6 41.9 reduce-scatter.22
where the time goes:
time: 747 us; the launch traced here: 742 us
  waiting for transfers between devices  530 us (71%)
  blocking collectives  101 us (14%)
  matrix products  46.8 us (6%)
  other arithmetic  36.6 us (5%)
  between operations  14.3 us (2%)
  local copies, waits for them, and re-layouts  12.5 us (2%)
    reduce_scatter x4, waiting for transfers between devices, scatter_units(): lax.psum_scatter(partial_value, 'row', scatter_dimension=1, tiled=True)  169 us
    reduce_scatter x4, waiting for transfers between devices, sum_tokens(): lax.psum_scatter(multiply(left_side, right_side), 'col', scatter_dimensio...  154 us
    all_gather x4, waiting for transfers between devices, gather_tokens(): return lax.all_gather(local_block, 'col', axis=0, tiled=True)  119 us
    all_gather x3, waiting for transfers between devices, gather_units(): return lax.all_gather(local_block, 'row', axis=1, tiled=True)  86 us
    psum x1, blocking collectives, per_device(): lax.psum((mixer_bias_part, first_gain_part, first_shift_part, narrow_bias...  59.1 us
    psum x4, blocking collectives, norm_sums(): return lax.psum((first_sum, second_sum), 'row')  19.7 us
  transfers between devices with their start and end apart: 16, of which 15 were waited for; matrix products, arithmetic and copies ran while one was open for 3% of the time, Pallas kernels for 0%

commit v1 on v0

v1 whole, which is shorter than its diff:
```python
import functools

import jax
import jax.numpy as jnp
from jax import lax
from jax.experimental import pallas as pl
from jax.experimental.pallas import tpu as pltpu
from jax.sharding import PartitionSpec as P

D = 1024
HD = 64


EPSILON = 1e-12
MASKED = -1e30


def product(left_side, right_side):
    return jnp.dot(left_side, right_side, preferred_element_type=jnp.float32)


def inner_rows(left_side, right_side):
    return lax.dot_general(
        left_side, right_side, (((0,), (0,)), ((), ())), preferred_element_type=jnp.float32
    )


def outer_back(left_side, right_side):
    return lax.dot_general(
        left_side, right_side, (((1,), (1,)), ((), ())), preferred_element_type=jnp.float32
    )


def gelu_exact(values):
    return jax.nn.gelu(values, approximate=False)


VMEM_BYTES = 32 * 1024 * 1024


def greet(me, count):
    barrier = pltpu.get_barrier_semaphore()

    @pl.when(me > 0)
    def _():
        pl.semaphore_signal(
            barrier, inc=1, device_id={"col": me - 1}, device_id_type=pl.DeviceIdType.MESH
        )

    @pl.when(me < count - 1)
    def _():
        pl.semaphore_signal(
            barrier, inc=1, device_id={"col": me + 1}, device_id_type=pl.DeviceIdType.MESH
        )

    inner = (me > 0) & (me < count - 1)

    @pl.when(inner)
    def _():
        pl.semaphore_wait(barrier, 2)

    @pl.when(jnp.logical_not(inner))
    def _():
        pl.semaphore_wait(barrier, 1)


def chain_gather(count, block_ref, out_ref, send_sem, recv_sem):
    me = lax.axis_index("col")
    greet(me, count)
    rows = block_ref.shape[0]

    def span(owner):
        return out_ref.at[pl.ds(pl.multiple_of(owner * rows, rows), rows)]

    def hop(source, owner, target, way, step):
        return pltpu.make_async_remote_copy(
            src_ref=source,
            dst_ref=span(owner),
            send_sem=send_sem.at[way, step],
            recv_sem=recv_sem.at[way, step],
            device_id={"col": target},
            device_id_type=pl.DeviceIdType.MESH,
        )

    for step in range(count - 1):

        @pl.when((me < count - 1) & (me - step >= 0))
        def _():
            source = block_ref if step == 0 else span(me - step)
            hop(source, me - step, me + 1, 0, step).start()

        @pl.when((me > 0) & (me + step <= count - 1))
        def _():
            source = block_ref if step == 0 else span(me + step)
            hop(source, me + step, me - 1, 1, step).start()

        if step == 0:
            out_ref[pl.ds(pl.multiple_of(me * rows, rows), rows), :] = block_ref[...]

        @pl.when(me - step - 1 >= 0)
        def _():
            hop(span(me - step - 1), me - step - 1, me, 0, step).wait_recv()

        @pl.when(me + step + 1 <= count - 1)
        def _():
            hop(span(me + step + 1), me + step + 1, me, 1, step).wait_recv()

    for step in range(count - 1):

        @pl.when((me < count - 1) & (me - step >= 0))
        def _():
            hop(span(me - step), me - step, me + 1, 0, step).wait_send()

        @pl.when((me > 0) & (me + step <= count - 1))
        def _():
            hop(span(me + step), me + step, me - 1, 1, step).wait_send()


def gather_tokens(block):
    count = lax.axis_size("col")
    rows, width = block.shape
    return pl.pallas_call(
        functools.partial(chain_gather, count),
        out_shape=jax.ShapeDtypeStruct((count * rows, width), block.dtype),
        in_specs=[pl.BlockSpec(memory_space=pltpu.VMEM)],
        out_specs=pl.BlockSpec(memory_space=pltpu.VMEM),
        scratch_shapes=[
            pltpu.SemaphoreType.DMA((2, count - 1)),
            pltpu.SemaphoreType.DMA((2, count - 1)),
        ],
        compiler_params=pltpu.CompilerParams(
            collective_id=0, has_side_effects=True, vmem_limit_bytes=VMEM_BYTES
        ),
        cost_estimate=pl.CostEstimate(
            flops=0, bytes_accessed=30 * 1024 * 1024, transcendentals=0
        ),
        name="chain_gather",
    )(block)


def chain_scatter(count, part_ref, out_ref, held, sent, send_sem, recv_sem):
    me = lax.axis_index("col")
    greet(me, count)
    rows = out_ref.shape[0]

    def mine(owner):
        return part_ref[pl.ds(pl.multiple_of(owner * rows, rows), rows), :].astype(jnp.float32)

    def hop(way, owner, target):
        return pltpu.make_async_remote_copy(
            src_ref=sent.at[way, owner],
            dst_ref=held.at[way, owner],
            send_sem=send_sem.at[way, owner],
            recv_sem=recv_sem.at[way, owner],
            device_id={"col": target},
            device_id_type=pl.DeviceIdType.MESH,
        )

    for step in range(count - 1):
        for way, owner, inside in (
            (0, count - 1 - step, me < count - 1 - step),
            (1, step, me > step),
        ):
            first = me == 0 if way == 0 else me == count - 1
            target = me + 1 if way == 0 else me - 1

            @pl.when(inside & first)
            def _():
                sent[way, owner] = mine(owner).astype(sent.dtype)
                hop(way, owner, target).start()

            @pl.when(inside & jnp.logical_not(first))
            def _():
                hop(way, owner, target).wait_recv()
                total = mine(owner) + held[way, owner].astype(jnp.float32)
                sent[way, owner] = total.astype(sent.dtype)
                hop(way, owner, target).start()

    out_ref[...] = mine(me)

    @pl.when(me > 0)
    def _():
        hop(0, me, me).wait_recv()
        out_ref[...] += held[0, me].astype(jnp.float32)

    @pl.when(me < count - 1)
    def _():
        hop(1, me, me).wait_recv()
        out_ref[...] += held[1, me].astype(jnp.float32)

    for step in range(count - 1):
        for way, owner, inside in (
            (0, count - 1 - step, me < count - 1 - step),
            (1, step, me > step),
        ):

            @pl.when(inside)
            def _():
                hop(way, owner, me).wait_send()


def scatter_tokens(part):
    count = lax.axis_size("col")
    rows, width = part.shape[0] // count, part.shape[1]
    return pl.pallas_call(
        functools.partial(chain_scatter, count),
        out_shape=jax.ShapeDtypeStruct((rows, width), jnp.float32),
        in_specs=[pl.BlockSpec(memory_space=pltpu.VMEM)],
        out_specs=pl.BlockSpec(memory_space=pltpu.VMEM),
        scratch_shapes=[
            pltpu.VMEM((2, count, rows, width), jnp.bfloat16),
            pltpu.VMEM((2, count, rows, width), jnp.bfloat16),
            pltpu.SemaphoreType.DMA((2, count)),
            pltpu.SemaphoreType.DMA((2, count)),
        ],
        compiler_params=pltpu.CompilerParams(
            collective_id=1, has_side_effects=True, vmem_limit_bytes=VMEM_BYTES
        ),
        cost_estimate=pl.CostEstimate(
            flops=0, bytes_accessed=30 * 1024 * 1024, transcendentals=0
        ),
        name="chain_scatter",
    )(part)


def slot_moves(swap):
    col_count = lax.axis_size("col")
    half = col_count // 2
    pairs = []
    for row in range(2):
        for col in range(col_count):
            there = (col // half) * col_count + 2 * (col % half) + (row ^ swap)
            pairs.append((row * col_count + col, there))
    return pairs


def to_slot_rows(stored):
    row, col = lax.axis_index("row"), lax.axis_index("col")
    rows = stored.shape[0] // 2
    landed = []
    for swap in range(2):
        block = lax.dynamic_slice_in_dim(stored, (row ^ swap) * rows, rows, 0)
        landed.append(lax.ppermute(block, ("row", "col"), slot_moves(swap)))
    odd = (col % 2) == 1
    left = jnp.where(odd, landed[1], landed[0])
    right = jnp.where(odd, landed[0], landed[1])
    return jnp.concatenate([left, right], axis=1)


def from_slot_rows(block):
    row, col = lax.axis_index("row"), lax.axis_index("col")
    width = block.shape[1] // 2
    landed = []
    for swap in range(2):
        piece = lax.dynamic_slice_in_dim(block, ((col % 2) ^ swap) * width, width, 1)
        pairs = [(there, here) for here, there in slot_moves(swap)]
        landed.append(lax.ppermute(piece, ("row", "col"), pairs))
    upper = jnp.where(row == 1, landed[1], landed[0])
    lower = jnp.where(row == 1, landed[0], landed[1])
    return jnp.concatenate([upper, lower], axis=0)


def norm_forward(summed, gain_row, shift_row):
    average = jnp.mean(summed, axis=1, keepdims=True)
    centred = summed - average
    variance = jnp.mean(centred * centred, axis=1, keepdims=True)
    inverse = lax.rsqrt(variance + EPSILON)
    normal = centred * inverse
    return (normal * gain_row + shift_row, normal, inverse)


def norm_backward(upstream, normal, inverse, gain_row):
    scaled = upstream * gain_row
    average = jnp.mean(scaled, axis=1, keepdims=True)
    crossed = jnp.mean(scaled * normal, axis=1, keepdims=True)
    return (scaled - average - normal * crossed) * inverse


def slot_scores(query_part, key_part, length):
    scores = jnp.einsum(
        "qhd,khd->hqk", query_part, key_part, preferred_element_type=jnp.float32
    ) * HD ** (-0.5)
    valid_keys = lax.iota(jnp.int32, key_part.shape[0]) < length
    return jnp.where(valid_keys[None, None, :], scores, MASKED)


def slot_forward(slot_item):
    query_part, key_part, value_part, length = slot_item
    scores = slot_scores(query_part, key_part, length)
    row_top = jnp.max(scores, axis=2, keepdims=True)
    exponent = jnp.exp(scores - row_top)
    row_total = jnp.sum(exponent, axis=2, keepdims=True)
    probabilities = (exponent / row_total).astype(jnp.bfloat16)
    mixed = jnp.einsum(
        "hqk,khd->qhd", probabilities, value_part, preferred_element_type=jnp.float32
    )
    return (mixed.astype(jnp.bfloat16), (row_top + jnp.log(row_total))[:, :, 0])


def slot_backward(slot_item):
    query_part, key_part, value_part, length, logsum, grad_heads = slot_item
    probabilities = jnp.exp(slot_scores(query_part, key_part, length) - logsum[:, :, None])
    grad_probs = jnp.einsum(
        "qhd,khd->hqk", grad_heads, value_part, preferred_element_type=jnp.float32
    )
    grad_values = jnp.einsum(
        "hqk,qhd->khd",
        probabilities.astype(jnp.bfloat16),
        grad_heads,
        preferred_element_type=jnp.float32,
    )
    along = jnp.sum(probabilities * grad_probs, axis=2, keepdims=True)
    grad_scores = (probabilities * (grad_probs - along)).astype(jnp.bfloat16)
    grad_query = jnp.einsum(
        "hqk,khd->qhd", grad_scores, key_part, preferred_element_type=jnp.float32
    ) * HD ** (-0.5)
    grad_keys = jnp.einsum(
        "hqk,qhd->khd", grad_scores, query_part, preferred_element_type=jnp.float32
    ) * HD ** (-0.5)
    return jnp.stack([grad_query, grad_keys, grad_values], axis=2)


def weight_total(part, dimension):
    part = lax.psum_scatter(
        part.astype(jnp.bfloat16), "row", scatter_dimension=dimension, tiled=True
    )
    return lax.psum(part, "dp").astype(jnp.float32)


def per_device(
    layer_input,
    lengths,
    attend_weight,
    attend_bias,
    mixer_weight,
    mixer_bias,
    first_gain,
    first_shift,
    widen_weight,
    widen_bias,
    narrow_weight,
    narrow_bias,
    second_gain,
    second_shift,
    cotangent,
):
    row_rank = lax.axis_index("row")
    col_rank = lax.axis_index("col")
    heads_here = attend_bias.shape[0]
    input_block = to_slot_rows(layer_input)
    block_rows = input_block.shape[0]
    length = lax.dynamic_index_in_dim(lengths, row_rank, 0, keepdims=False)
    vectors = jnp.stack(
        [mixer_bias, first_gain, first_shift, narrow_bias, second_gain, second_shift]
    )
    vectors = lax.all_gather(vectors, "row", axis=1, tiled=True)
    mixer_bias, first_gain, first_shift, narrow_bias, second_gain, second_shift = vectors
    attend_weight = lax.all_gather(attend_weight, "row", axis=0, tiled=True)
    mixer_weight = lax.all_gather(mixer_weight, "row", axis=1, tiled=True)
    widen_weight = lax.all_gather(widen_weight, "row", axis=0, tiled=True)
    narrow_weight = lax.all_gather(narrow_weight, "row", axis=1, tiled=True)

    gathered_input = gather_tokens(input_block)
    slot_rows = gathered_input.shape[0]
    bias_full = jnp.concatenate(
        [attend_bias[:, :HD], jnp.zeros((heads_here, HD), jnp.float32), attend_bias[:, HD:]],
        axis=1,
    ).reshape(heads_here * 3 * HD)
    packed = (product(gathered_input, attend_weight) + bias_full).astype(jnp.bfloat16)
    split_heads = packed.reshape(slot_rows, heads_here, 3, HD)
    query_all = split_heads[:, :, 0]
    keys_all = split_heads[:, :, 1]
    values_all = split_heads[:, :, 2]
    mixed, logsum = slot_forward((query_all, keys_all, values_all, length))
    mixed_block = mixed.reshape(slot_rows, heads_here * HD)
    attended = scatter_tokens(product(mixed_block, mixer_weight)) + mixer_bias
    first_out, first_normal, first_inverse = norm_forward(
        input_block.astype(jnp.float32) + attended, first_gain, first_shift
    )
    gathered_first = gather_tokens(first_out.astype(jnp.bfloat16))
    widened = product(gathered_first, widen_weight) + widen_bias
    active, gelu_pull = jax.vjp(gelu_exact, widened)
    active_block = active.astype(jnp.bfloat16)
    narrowed = scatter_tokens(product(active_block, narrow_weight)) + narrow_bias
    second_out, second_normal, second_inverse = norm_forward(
        first_out + narrowed, second_gain, second_shift
    )
    layer_output = from_slot_rows(second_out.astype(jnp.bfloat16))
    positions = col_rank * block_rows + lax.iota(jnp.int32, block_rows)
    upstream = jnp.where(
        (positions < length)[:, None], to_slot_rows(cotangent).astype(jnp.float32), 0.0
    )
    second_gain_part = jnp.sum(upstream * second_normal, axis=0)
    second_shift_part = jnp.sum(upstream, axis=0)
    grad_second = norm_backward(upstream, second_normal, second_inverse, second_gain)
    grad_narrowed = grad_second.astype(jnp.bfloat16)
    narrow_bias_part = jnp.sum(grad_narrowed, axis=0, dtype=jnp.float32)
    grad_narrow_block = gather_tokens(grad_narrowed)
    narrow_total = weight_total(inner_rows(active_block, grad_narrow_block), 1)
    grad_active = outer_back(grad_narrow_block, narrow_weight)
    grad_widened = gelu_pull(grad_active)[0].astype(jnp.bfloat16)
    widen_bias_part = jnp.sum(grad_widened, axis=0, dtype=jnp.float32)
    grad_first = scatter_tokens(outer_back(grad_widened, widen_weight)) + grad_second
    widen_total = weight_total(inner_rows(gathered_first, grad_widened), 0)
    first_gain_part = jnp.sum(grad_first * first_normal, axis=0)
    first_shift_part = jnp.sum(grad_first, axis=0)
    grad_attended = norm_backward(grad_first, first_normal, first_inverse, first_gain)
    grad_mix = grad_attended.astype(jnp.bfloat16)
    mixer_bias_part = jnp.sum(grad_mix, axis=0, dtype=jnp.float32)
    grad_mixer_block = gather_tokens(grad_mix)
    mixer_total = weight_total(inner_rows(mixed_block, grad_mixer_block), 1)
    grad_mixed = outer_back(grad_mixer_block, mixer_weight).astype(jnp.bfloat16)
    grad_heads = grad_mixed.reshape(slot_rows, heads_here, HD)
    grad_slots = slot_backward((query_all, keys_all, values_all, length, logsum, grad_heads))
    grad_packed = grad_slots.reshape(slot_rows, heads_here * 3 * HD).astype(jnp.bfloat16)
    packed_sums = jnp.sum(grad_packed, axis=0, dtype=jnp.float32).reshape(heads_here, 3, HD)
    attend_bias_part = jnp.concatenate([packed_sums[:, 0], packed_sums[:, 2]], axis=1)
    attend_total = weight_total(inner_rows(gathered_input, grad_packed), 0)
    input_gradient = scatter_tokens(outer_back(grad_packed, attend_weight)) + grad_attended
    input_gradient = from_slot_rows(input_gradient)
    column_totals = lax.psum((attend_bias_part, widen_bias_part), ("dp", "row"))
    vector_parts = jnp.stack(
        [
            mixer_bias_part,
            first_gain_part,
            first_shift_part,
            narrow_bias_part,
            second_gain_part,
            second_shift_part,
        ]
    )
    half = vector_parts.shape[1] // 2
    vector_totals = lax.dynamic_slice_in_dim(
        lax.psum(vector_parts, ("dp", "row", "col")), row_rank * half, half, 1
    )
    return (
        layer_output,
        input_gradient,
        attend_total,
        column_totals[0],
        mixer_total,
        vector_totals[0],
        vector_totals[1],
        vector_totals[2],
        widen_total,
        column_totals[1],
        narrow_total,
        vector_totals[3],
        vector_totals[4],
        vector_totals[5],
    )


def solution(mesh):
    return jax.shard_map(
        per_device,
        mesh=mesh,
        in_specs=(
            P(("dp", "col"), "row"),
            P("dp"),
            P("row", "col"),
            P("col", None),
            P("col", "row"),
            P("row"),
            P("row"),
            P("row"),
            P("row", "col"),
            P("col"),
            P("col", "row"),
            P("row"),
            P("row"),
            P("row"),
            P(("dp", "col"), "row"),
        ),
        out_specs=(
            P(("dp", "col"), "row"),
            P(("dp", "col"), "row"),
            P("row", "col"),
            P("col", None),
            P("col", "row"),
            P("row"),
            P("row"),
            P("row"),
            P("row", "col"),
            P("col"),
            P("col", "row"),
            P("row"),
            P("row"),
            P("row"),
        ),
        check_vma=False,
    )
```

time: 747 us -> 451 us (0.60)
  waiting for transfers between devices: 530 us -> 92.8 us
  Pallas kernels: 0 us -> 177 us
  blocking collectives: 101 us -> 73.5 us
  starting transfers between devices: 0.84 us -> 26.7 us
  other arithmetic: 36.6 us -> 16.2 us
  matrix products: 46.8 us -> 38.8 us
    reduce_scatter x8 -> x4, waiting for transfers between devices: 323 us -> 91.2 us  [weight_total(): lax.psum_scatter(part.astype(jnp.bfloat16), 'row', scatter_dimension=dime...]
    all_gather x7 -> x3, waiting for transfers between devices: 206 us -> 0.04 us  [the longest x1 0.02 us: per_device(): attend_weight = lax.all_gather(attend_weight, 'row', axis=0, tiled=True)]
    pallas_call x0 -> x8, Pallas kernels: none -> 177 us  [the longest x4 109 us: scatter_tokens(): pl.pallas_call(functools.partial(chain_scatter, count), out_shape=jax.Sha...]
    psum x6 -> x2, blocking collectives: 92.3 us -> 54.3 us  [the longest x1 40 us: per_device(): lax.psum(vector_parts, ('dp', 'row', 'col'))]
    ppermute x0 -> x8, starting transfers between devices: none -> 26.2 us  [the longest x4 15.2 us: from_slot_rows(): landed.append(lax.ppermute(piece, ('row', 'col'), pairs))]
    all_gather x1 -> x2, blocking collectives: 8.73 us -> 19.2 us  [the longest x1 14.4 us: per_device(): mixer_weight = lax.all_gather(mixer_weight, 'row', axis=1, tiled=True)]
    dot_general x4, matrix products: 13.7 us -> 6.14 us  [outer_back(): lax.dot_general(left_side, right_side, (((1,), (1,)), ((), ())), preferre...]
  transfers between devices with their start and end apart: 16 -> 16, of which waited for: 15 -> 3; matrix products, arithmetic and copies ran while one was open for 3% -> 9% of each run, Pallas kernels for 0% -> 20%
where the time goes in v1:
time: 451 us; the launch traced here: 449 us
  Pallas kernels  177 us (39%)
  waiting for transfers between devices  92.8 us (21%)
  blocking collectives  73.5 us (16%)
  matrix products  38.8 us (9%)
  starting transfers between devices  26.7 us (6%)
  other arithmetic  16.2 us (4%)
  between operations  15 us (3%)
  local copies, waits for them, and re-layouts  9.41 us (2%)
    pallas_call x4, Pallas kernels, scatter_tokens(): pl.pallas_call(functools.partial(chain_scatter, count), out_shape=jax.Sha...  109 us
    reduce_scatter x4, waiting for transfers between devices, weight_total(): lax.psum_scatter(part.astype(jnp.bfloat16), 'row', scatter_dimension=dime...  91.2 us
    pallas_call x4, Pallas kernels, gather_tokens(): pl.pallas_call(functools.partial(chain_gather, count), out_shape=jax.Shap...  68.1 us
    psum x1, blocking collectives, per_device(): lax.psum(vector_parts, ('dp', 'row', 'col'))  40 us
    dot_general x4, matrix products, product(): return jnp.dot(left_side, right_side, preferred_element_type=jnp.float32)  15.6 us
    ppermute x4, starting transfers between devices, from_slot_rows(): landed.append(lax.ppermute(piece, ('row', 'col'), pairs))  15.2 us
    all_gather x1, blocking collectives, per_device(): mixer_weight = lax.all_gather(mixer_weight, 'row', axis=1, tiled=True)  14.4 us
    psum x1, blocking collectives, per_device(): column_totals = lax.psum((attend_bias_part, widen_bias_part), ('dp', 'row'))  14.4 us
  transfers between devices with their start and end apart: 16, of which 3 were waited for; matrix products, arithmetic and copies ran while one was open for 9% of the time, Pallas kernels for 20%

profile of v1, /device:TPU:8, one launch (start us, length us, event | category | flops | bytes accessed | tf_op | source)
XLA Modules:
  0.0 449.1 jit_solution(8256729270823426210)
XLA Ops:
  9.8 2.6 collective-permute-start
  12.5 2.3 collective-permute-start.1
  16.2 4.6 %collective-permute-start.5 = (bf16[128,512]{1,0:T(8,128)(2,1)S(1)}, bf16[128,512]{1,0:T(8,128)(2,1)S(1)}, u32[]{:S(2)}, u32[]{:S(2)}) collective-permute-start(bf16[128,512]{1,0:T(8,128)(2,1)S(1)} %get-tuple-element.53), channel_id=1, source_target_pairs={{0,0},{1,2},{2,4},{3,6},{4,1},{5,3},{6,5},{7,7},{8,8},{9,10},{10,1... | collective-permute-start | bytes 393224 | tf_op jit(solution)/shard_map/ppermute | solution.py:243
  23.1 4.7 %all_gather.17 = f32[6,1024]{1,0:T(8,128)S(1)} all-gather(f32[6,512]{1,0:T(8,128)S(1)} %stack.60), channel_id=1, replica_groups=mesh['dp'=4,'row'=2,'col'=4] {'row'}, dimensions={1}, use_global_device_ids=true | all-gather | bytes 36864 | tf_op jit(solution)/shard_map/all_gather | solution.py:356
  27.9 14.4 %all_gather.16 = bf16[256,1024]{1,0:T(8,128)(2,1)S(1)} all-gather(bf16[256,512]{1,0:T(8,128)(2,1)S(1)} %copy-done.16), channel_id=1, replica_groups=mesh['dp'=4,'row'=2,'col'=4] {'row'}, dimensions={1}, use_global_device_ids=true | all-gather | bytes 786432 | tf_op jit(solution)/shard_map/all_gather | solution.py:359
  42.4 17.7 %chain_gather.4 = bf16[512,1024]{1,0:T(8,128)(2,1)S(1)} custom-call(bf16[128,1024]{1,0:T(8,128)(2,1)S(1)} %pad_maximum_fusion.1.block_ref), custom_call_target="tpu_custom_call" | custom-call | bytes 31457280 | tf_op jit(solution)/shard_map/chain_gather/pallas_call | solution.py:122
  60.2 3.3 add_convert_fusion.1
  69.2 26.7 %chain_scatter.4 = f32[128,1024]{1,0:T(8,128)S(1)} custom-call(f32[512,1024]{1,0:T(8,128)S(1)} %fusion.30.part_ref), custom_call_target="tpu_custom_call" | custom-call | bytes 31457280 | tf_op jit(solution)/shard_map/chain_scatter/pallas_call | solution.py:205
  96.4 17.3 %chain_gather.5 = bf16[512,1024]{1,0:T(8,128)(2,1)S(1)} custom-call(bf16[128,1024]{1,0:T(8,128)(2,1)S(1)} %fusion.21.block_ref), custom_call_target="tpu_custom_call" | custom-call | bytes 31457280 | tf_op jit(solution)/shard_map/chain_gather/pallas_call | solution.py:122
  113.8 8.7 %multiply_convert_fusion.1 = (bf16[512,1024]{1,0:T(8,128)(2,1)}, f32[512,1024]{1,0:T(8,128)}, f32[512,1024]{1,0:T(8,128)}) fusion(f32[1024]{0:T(1024)S(1)} %copy-done.27, bf16[512,1024]{1,0:T(8,128)(2,1)S(1)} %chain_gather.5, bf16[1024,1024]{1,0:T(8,128)(2,1)} %all-gather.6.cloned.1.call-done), kind=kOutput, calls=%fused_computation.14 | convolution fusion | flops 1108344832 | bytes 8392704 | tf_op jit(solution)/shard_map/dot_general | solution.py:19
  122.6 3.2 fusion.31.part_ref
  125.8 28.0 %chain_scatter.5 = f32[128,1024]{1,0:T(8,128)S(1)} custom-call(f32[512,1024]{1,0:T(8,128)S(1)} %fusion.31.part_ref), custom_call_target="tpu_custom_call" | custom-call | bytes 31457280 | tf_op jit(solution)/shard_map/chain_scatter/pallas_call | solution.py:205
  155.7 15.8 %chain_gather.6 = bf16[512,1024]{1,0:T(8,128)(2,1)S(1)} custom-call(bf16[128,1024]{1,0:T(8,128)(2,1)S(1)} %get-tuple-element.29.block_ref), custom_call_target="tpu_custom_call" | custom-call | bytes 31457280 | tf_op jit(solution)/shard_map/chain_gather/pallas_call | solution.py:122
  171.5 1.9 convert_reduce_fusion
  175.7 24.6 %chain_scatter.6 = f32[128,1024]{1,0:T(8,128)S(1)} custom-call(f32[512,1024]{1,0:T(8,128)S(1)} %fusion.32.part_ref), custom_call_target="tpu_custom_call" | custom-call | bytes 31457280 | tf_op jit(solution)/shard_map/chain_scatter/pallas_call | solution.py:205
  201.7 17.2 %chain_gather.7 = bf16[512,1024]{1,0:T(8,128)(2,1)S(1)} custom-call(bf16[128,1024]{1,0:T(8,128)(2,1)S(1)} %get-tuple-element.32.block_ref), custom_call_target="tpu_custom_call" | custom-call | bytes 31457280 | tf_op jit(solution)/shard_map/chain_gather/pallas_call | solution.py:122
  220.8 3.4 multiply_reduce_fusion
  228.6 2.2 convolution_convert_fusion.2
  230.9 3.8 convolution_convert_fusion
  236.0 2.6 convolution_convert_fusion.1
  239.6 2.6 collective-permute-start.2
  242.1 1.9 collective-permute-start.3
  244.1 21.1 %reduce-scatter.5.cloned.1.call-done = bf16[512,768]{1,0:T(8,128)(2,1)} async-done(((bf16[1024,768]{1,0:T(8,128)(2,1)}), bf16[512,768]{1,0:T(8,128)(2,1)}) %reduce-scatter.5.cloned.1.call-update) | async-done | bytes 786448 | tf_op jit(solution)/shard_map/reduce_scatter | solution.py:324
  265.2 35.3 %reduce-scatter.11.cloned.1.call-done = bf16[1024,512]{1,0:T(8,128)(2,1)} async-done(((bf16[1024,1024]{1,0:T(8,128)(2,1)}), bf16[1024,512]{1,0:T(8,128)(2,1)}) %reduce-scatter.11.cloned.1.call-update) | async-done | bytes 1048592 | tf_op jit(solution)/shard_map/reduce_scatter | solution.py:324
  300.5 34.8 %reduce-scatter.9.cloned.1.call-done = bf16[512,1024]{1,0:T(8,128)(2,1)} async-done(((bf16[1024,1024]{1,0:T(8,128)(2,1)}), bf16[512,1024]{1,0:T(8,128)(2,1)}) %reduce-scatter.9.cloned.1.call-update) | async-done | bytes 1048592 | tf_op jit(solution)/shard_map/reduce_scatter | solution.py:324
  335.3 2.4 fusion.33.part_ref
  337.7 29.3 %chain_scatter.7 = f32[128,1024]{1,0:T(8,128)S(1)} custom-call(f32[512,1024]{1,0:T(8,128)S(1)} %fusion.33.part_ref), custom_call_target="tpu_custom_call" | custom-call | bytes 31457280 | tf_op jit(solution)/shard_map/chain_scatter/pallas_call | solution.py:205
  367.2 2.6 collective-permute-start.6
  369.8 8.2 %collective-permute-start.7 = (f32[128,512]{1,0:T(8,128)S(1)}, f32[128,512]{1,0:T(8,128)S(1)}, u32[]{:S(2)}, u32[]{:S(2)}) collective-permute-start(f32[128,512]{1,0:T(8,128)S(1)} %get-tuple-element.49), channel_id=1, source_target_pairs={{0,0},{2,1},{4,2},{6,3},{1,4},{3,5},{5,6},{7,7},{8,8},{10,9},{12,1... | collective-permute-start | bytes 786440 | tf_op jit(solution)/shard_map/ppermute | solution.py:257
  378.1 14.4 %all-reduce = (f32[4,128]{1,0:T(4,128)}, f32[1024]{0:T(1024)}) all-reduce(f32[4,128]{1,0:T(4,128)S(1)} %pad_maximum_fusion.5, f32[1024]{0:T(1024)S(1)} %get-tuple-element.34), channel_id=1, replica_groups=mesh['dp'=4,'row'=2,'col'=4] {'dp','row'}, use_global_device_ids=true, to_apply=%region_14.15 | all-reduce | flops 1536 | bytes 12288 | tf_op jit(solution)/shard_map/psum | solution.py:421
  392.4 40.0 %psum.52 = f32[6,1024]{1,0:T(8,128)S(1)} all-reduce(f32[6,1024]{1,0:T(8,128)S(1)} %stack.71), channel_id=1, replica_groups=mesh['dp'=4,'row'=2,'col'=4] {'dp','row','col'}, use_global_device_ids=true, to_apply=%region_23.24 | all-reduce | flops 6144 | bytes 49152 | tf_op jit(solution)/shard_map/psum | solution.py:434
  436.7 2.4 convert_element_type.107
  (156 shorter events, 34.0 us)
Async XLA Ops:
  7.2 15.9 %copy-start.24 = (f32[512]{0:T(512)S(1)}, f32[512]{0:T(512)}, u32[]{:S(2)}) copy-start(f32[512]{0:T(512)} %param.28) | copy-start | bytes 6148
  7.2 15.8 %copy-start.23 = (f32[512]{0:T(512)S(1)}, f32[512]{0:T(512)}, u32[]{:S(2)}) copy-start(f32[512]{0:T(512)} %param.27) | copy-start | bytes 6148
  7.2 15.8 %copy-start.22 = (f32[512]{0:T(512)S(1)}, f32[512]{0:T(512)}, u32[]{:S(2)}) copy-start(f32[512]{0:T(512)} %param.26) | copy-start | bytes 6148
  7.3 20.6 %copy-start.16 = (bf16[256,512]{1,0:T(8,128)(2,1)S(1)}, bf16[256,512]{1,0:T(8,128)(2,1)}, u32[]{:S(2)}) copy-start(bf16[256,512]{1,0:T(8,128)(2,1)} %param.19) | copy-start | bytes 786436
  7.3 52.9 %all-gather.4.cloned.1.call-start = ((), (), s32[]{:S(2)}) async-start(), calls=%async_computation.4 | async-start | bytes 2359296 | tf_op jit(solution)/shard_map/all_gather | solution.py:358
  8.0 105.8 %all-gather.6.cloned.1.call-start = ((), (), s32[]{:S(2)}) async-start(), calls=%async_computation.5 | async-start | bytes 3145728 | tf_op jit(solution)/shard_map/all_gather | solution.py:360
  8.8 113.8 %all-gather.8.cloned.1.call-start = ((), (), s32[]{:S(2)}) async-start(), calls=%async_computation.6 | async-start | bytes 3145728 | tf_op jit(solution)/shard_map/all_gather | solution.py:361
  9.8 32.5 %collective-permute-start = (bf16[128,512]{1,0:T(8,128)(2,1)S(1)}, bf16[128,512]{1,0:T(8,128)(2,1)S(1)}, u32[]{:S(2)}, u32[]{:S(2)}) collective-permute-start(bf16[128,512]{1,0:T(8,128)(2,1)S(1)} %get-tuple-element.60), channel_id=1, source_target_pairs={{0,1},{1,3},{2,5},{3,7},{4,0},{5,2},{6,4},{7,6},{8,9},{9,11},{10,1... | collective-permute-start | bytes 393224 | tf_op jit(solution)/shard_map/ppermute | solution.py:243
  12.5 29.9 %collective-permute-start.1 = (bf16[128,512]{1,0:T(8,128)(2,1)S(1)}, bf16[128,512]{1,0:T(8,128)(2,1)S(1)}, u32[]{:S(2)}, u32[]{:S(2)}) collective-permute-start(bf16[128,512]{1,0:T(8,128)(2,1)S(1)} %get-tuple-element.61), channel_id=1, source_target_pairs={{0,0},{1,2},{2,4},{3,6},{4,1},{5,3},{6,5},{7,7},{8,8},{9,10},{10,1... | collective-permute-start | bytes 393224 | tf_op jit(solution)/shard_map/ppermute | solution.py:243
  14.8 45.3 %collective-permute-start.4 = (bf16[128,512]{1,0:T(8,128)(2,1)S(1)}, bf16[128,512]{1,0:T(8,128)(2,1)S(1)}, u32[]{:S(2)}, u32[]{:S(2)}) collective-permute-start(bf16[128,512]{1,0:T(8,128)(2,1)S(1)} %get-tuple-element.52), channel_id=1, source_target_pairs={{0,1},{1,3},{2,5},{3,7},{4,0},{5,2},{6,4},{7,6},{8,9},{9,11},{10,1... | collective-permute-start | bytes 393224 | tf_op jit(solution)/shard_map/ppermute | solution.py:243
  16.2 44.0 %collective-permute-start.5 = (bf16[128,512]{1,0:T(8,128)(2,1)S(1)}, bf16[128,512]{1,0:T(8,128)(2,1)S(1)}, u32[]{:S(2)}, u32[]{:S(2)}) collective-permute-start(bf16[128,512]{1,0:T(8,128)(2,1)S(1)} %get-tuple-element.53), channel_id=1, source_target_pairs={{0,0},{1,2},{2,4},{3,6},{4,1},{5,3},{6,5},{7,7},{8,8},{9,10},{10,1... | collective-permute-start | bytes 393224 | tf_op jit(solution)/shard_map/ppermute | solution.py:243
  20.8 223.2 %reduce-scatter.7.cloned.1.call-start = ((), (), s32[]{:S(2)}) async-start(), calls=%async_computation.8 | async-start | bytes 786432 | tf_op jit(solution)/shard_map/reduce_scatter | solution.py:324
  42.3 26.4 %copy-start.7 = (bf16[256,1024]{1,0:T(8,128)(2,1)}, bf16[256,1024]{1,0:T(8,128)(2,1)S(1)}, u32[]{:S(2)}) copy-start(bf16[256,1024]{1,0:T(8,128)(2,1)S(1)} %all_gather.16) | copy-start | bytes 1572868
  68.7 27.1 %copy-start.12 = (bf16[4,64,512]{2,1,0:T(8,128)(2,1)}, bf16[4,64,512]{2,1,0:T(8,128)(2,1)S(1)}, u32[]{:S(2)}) copy-start(bf16[4,64,512]{2,1,0:T(8,128)(2,1)S(1)} %fusion.17) | copy-start | bytes 786436
  95.8 18.0 %copy-start.27 = (f32[1024]{0:T(1024)S(1)}, f32[1024]{0:T(1024)}, u32[]{:S(2)}) copy-start(f32[1024]{0:T(1024)} %param.24) | copy-start | bytes 12292
  96.0 57.8 %copy-start.2 = (f32[128,1024]{1,0:T(8,128)}, f32[128,1024]{1,0:T(8,128)S(1)}, u32[]{:S(2)}) copy-start(f32[128,1024]{1,0:T(8,128)S(1)} %get-tuple-element.44) | copy-start | bytes 1572868
  125.7 45.7 %copy-start.32 = (f32[512,1024]{1,0:T(8,128)S(1)}, f32[512,1024]{1,0:T(8,128)}, u32[]{:S(2)}) copy-start(f32[512,1024]{1,0:T(8,128)} %get-tuple-element.80) | copy-start | bytes 6291460
  154.1 17.4 %copy-start.31 = (f32[512,1024]{1,0:T(8,128)S(1)}, f32[512,1024]{1,0:T(8,128)}, u32[]{:S(2)}) copy-start(f32[512,1024]{1,0:T(8,128)} %get-tuple-element.42) | copy-start | bytes 6291460
  154.3 17.2 %copy-start.26 = (bf16[1024,1024]{1,0:T(8,128)(2,1)S(1)}, bf16[1024,1024]{1,0:T(8,128)(2,1)}, u32[]{:S(2)}) copy-start(bf16[1024,1024]{1,0:T(8,128)(2,1)} %all-gather.8.cloned.1.call-done) | copy-start | bytes 6291460
  175.7 24.6 %copy-start.3 = (f32[128,1024]{1,0:T(8,128)S(1)}, f32[128,1024]{1,0:T(8,128)}, u32[]{:S(2)}) copy-start(f32[128,1024]{1,0:T(8,128)} %copy-done.2) | copy-start | bytes 1572868
  200.6 18.3 %copy-start.8 = (bf16[256,1024]{1,0:T(8,128)(2,1)S(1)}, bf16[256,1024]{1,0:T(8,128)(2,1)}, u32[]{:S(2)}) copy-start(bf16[256,1024]{1,0:T(8,128)(2,1)} %copy-done.7) | copy-start | bytes 1572868
  200.7 18.8 %copy-start.13 = (bf16[4,64,512]{2,1,0:T(8,128)(2,1)S(1)}, bf16[4,64,512]{2,1,0:T(8,128)(2,1)}, u32[]{:S(2)}) copy-start(bf16[4,64,512]{2,1,0:T(8,128)(2,1)} %copy-done.12) | copy-start | bytes 786436
  220.7 44.5 %reduce-scatter.5.cloned.1.call-start = ((), (), s32[]{:S(2)}) async-start(), calls=%async_computation.7 | async-start | bytes 2359296 | tf_op jit(solution)/shard_map/reduce_scatter | solution.py:324
  230.9 69.6 %reduce-scatter.11.cloned.1.call-start = ((), (), s32[]{:S(2)}) async-start(), calls=%async_computation.10 | async-start | bytes 3145728 | tf_op jit(solution)/shard_map/reduce_scatter | solution.py:324
  234.8 100.5 %reduce-scatter.9.cloned.1.call-start = ((), (), s32[]{:S(2)}) async-start(), calls=%async_computation.9 | async-start | bytes 3145728 | tf_op jit(solution)/shard_map/reduce_scatter | solution.py:324
  238.6 96.7 %copy-start.15 = (bf16[512,4,3,64]{0,3,2,1:T(8,128)(2,1)S(1)}, bf16[512,4,3,64]{0,3,2,1:T(8,128)(2,1)}, u32[]{:S(2)}) copy-start(bf16[512,4,3,64]{0,3,2,1:T(8,128)(2,1)} %copy-done.14) | copy-start | bytes 2359300
  238.6 196.1 %all-reduce.4.cloned.1.call-start = ((), (), s32[]{:S(2)}) async-start(), calls=%async_computation.11 | async-start | bytes 6291456 | tf_op jit(solution)/shard_map/psum | solution.py:327
  239.6 193.6 %collective-permute-start.2 = (bf16[128,512]{1,0:T(8,128)(2,1)S(1)}, bf16[128,512]{1,0:T(8,128)(2,1)S(1)}, u32[]{:S(2)}, u32[]{:S(2)}) collective-permute-start(bf16[128,512]{1,0:T(8,128)(2,1)S(1)} %get-tuple-element.56), channel_id=1, source_target_pairs={{1,0},{3,1},{5,2},{7,3},{0,4},{2,5},{4,6},{6,7},{9,8},{11,9},{13,1... | collective-permute-start | bytes 393224 | tf_op jit(solution)/shard_map/ppermute | solution.py:257
  242.1 191.0 %collective-permute-start.3 = (bf16[128,512]{1,0:T(8,128)(2,1)S(1)}, bf16[128,512]{1,0:T(8,128)(2,1)S(1)}, u32[]{:S(2)}, u32[]{:S(2)}) collective-permute-start(bf16[128,512]{1,0:T(8,128)(2,1)S(1)} %get-tuple-element.57), channel_id=1, source_target_pairs={{0,0},{2,1},{4,2},{6,3},{1,4},{3,5},{5,6},{7,7},{8,8},{10,9},{12,1... | collective-permute-start | bytes 393224 | tf_op jit(solution)/shard_map/ppermute | solution.py:257
  337.7 29.3 %copy-start.6 = (f32[128,1024]{1,0:T(8,128)S(1)}, f32[128,1024]{1,0:T(8,128)}, u32[]{:S(2)}) copy-start(f32[128,1024]{1,0:T(8,128)} %get-tuple-element.33) | copy-start | bytes 1572868
  367.2 66.7 %collective-permute-start.6 = (f32[128,512]{1,0:T(8,128)S(1)}, f32[128,512]{1,0:T(8,128)S(1)}, u32[]{:S(2)}, u32[]{:S(2)}) collective-permute-start(f32[128,512]{1,0:T(8,128)S(1)} %get-tuple-element.48), channel_id=1, source_target_pairs={{1,0},{3,1},{5,2},{7,3},{0,4},{2,5},{4,6},{6,7},{9,8},{11,9},{13,1... | collective-permute-start | bytes 786440 | tf_op jit(solution)/shard_map/ppermute | solution.py:257
  369.8 64.1 %collective-permute-start.7 = (f32[128,512]{1,0:T(8,128)S(1)}, f32[128,512]{1,0:T(8,128)S(1)}, u32[]{:S(2)}, u32[]{:S(2)}) collective-permute-start(f32[128,512]{1,0:T(8,128)S(1)} %get-tuple-element.49), channel_id=1, source_target_pairs={{0,0},{2,1},{4,2},{6,3},{1,4},{3,5},{5,6},{7,7},{8,8},{10,9},{12,1... | collective-permute-start | bytes 786440 | tf_op jit(solution)/shard_map/ppermute | solution.py:257
  (17 other events, 105.5 us)
Sparse Core Ops, SparseCore 0:
  9.7 36.8 all-gather.3
  48.1 33.8 all-gather.5
  83.5 33.1 all-gather.7
  220.8 14.0 reduce-scatter.6
  237.7 27.4 reduce-scatter.4
  267.8 32.6 reduce-scatter.10
  303.4 31.8 reduce-scatter.8
  337.8 69.8 all-reduce.3

commit v2 on v1

--- a/solution.py
+++ b/solution.py
@@ -35,38 +35,54 @@
     return jax.nn.gelu(values, approximate=False)
 
 
-VMEM_BYTES = 32 * 1024 * 1024
-
-
-def greet(me, count):
+VMEM_BYTES = 48 * 1024 * 1024
+MESH = pl.DeviceIdType.MESH
+
+
+def reduce_levels(dp_count):
+    levels = [("dp", 1), ("row", 1)]
+    bit = 2
+    while bit < dp_count:
+        levels.append(("dp", bit))
+        bit *= 2
+    return levels
+
+
+def greet(me, count, levels, whole_chain):
     barrier = pltpu.get_barrier_semaphore()
+    for axis, bit in levels:
+        pl.semaphore_signal(
+            barrier, inc=1, device_id={axis: lax.axis_index(axis) ^ bit}, device_id_type=MESH
+        )
+    if whole_chain:
+        for step in range(1, count):
+            pl.semaphore_signal(
+                barrier, inc=1, device_id={"col": lax.rem(me + step, count)}, device_id_type=MESH
+            )
+        pl.semaphore_wait(barrier, len(levels) + count - 1)
+        return
 
     @pl.when(me > 0)
     def _():
-        pl.semaphore_signal(
-            barrier, inc=1, device_id={"col": me - 1}, device_id_type=pl.DeviceIdType.MESH
-        )
+        pl.semaphore_signal(barrier, inc=1, device_id={"col": me - 1}, device_id_type=MESH)
 
     @pl.when(me < count - 1)
     def _():
-        pl.semaphore_signal(
-            barrier, inc=1, device_id={"col": me + 1}, device_id_type=pl.DeviceIdType.MESH
-        )
+        pl.semaphore_signal(barrier, inc=1, device_id={"col": me + 1}, device_id_type=MESH)
 
     inner = (me > 0) & (me < count - 1)
 
     @pl.when(inner)
     def _():
-        pl.semaphore_wait(barrier, 2)
+        pl.semaphore_wait(barrier, len(levels) + 2)
 
     @pl.when(jnp.logical_not(inner))
     def _():
-        pl.semaphore_wait(barrier, 1)
-
-
-def chain_gather(count, block_ref, out_ref, send_sem, recv_sem):
+        pl.semaphore_wait(barrier, len(levels) + 1)
+
+
+def gather_stages(count, block_ref, out_ref, send_sem, recv_sem):
     me = lax.axis_index("col")
-    greet(me, count)
     rows = block_ref.shape[0]
 
     def span(owner):
@@ -79,11 +95,10 @@
             send_sem=send_sem.at[way, step],
             recv_sem=recv_sem.at[way, step],
             device_id={"col": target},
-            device_id_type=pl.DeviceIdType.MESH,
-        )
-
-    for step in range(count - 1):
-
+            device_id_type=MESH,
+        )
+
+    def start(step):
         @pl.when((me < count - 1) & (me - step >= 0))
         def _():
             source = block_ref if step == 0 else span(me - step)
@@ -97,6 +112,7 @@
         if step == 0:
             out_ref[pl.ds(pl.multiple_of(me * rows, rows), rows), :] = block_ref[...]
 
+    def arrive(step):
         @pl.when(me - step - 1 >= 0)
         def _():
             hop(span(me - step - 1), me - step - 1, me, 0, step).wait_recv()
@@ -105,42 +121,31 @@
         def _():
             hop(span(me + step + 1), me + step + 1, me, 1, step).wait_recv()
 
-    for step in range(count - 1):
-
-        @pl.when((me < count - 1) & (me - step >= 0))
-        def _():
-            hop(span(me - step), me - step, me + 1, 0, step).wait_send()
-
-        @pl.when((me > 0) & (me + step <= count - 1))
-        def _():
-            hop(span(me + step), me + step, me - 1, 1, step).wait_send()
-
-
-def gather_tokens(block):
-    count = lax.axis_size("col")
-    rows, width = block.shape
-    return pl.pallas_call(
-        functools.partial(chain_gather, count),
-        out_shape=jax.ShapeDtypeStruct((count * rows, width), block.dtype),
-        in_specs=[pl.BlockSpec(memory_space=pltpu.VMEM)],
-        out_specs=pl.BlockSpec(memory_space=pltpu.VMEM),
-        scratch_shapes=[
-            pltpu.SemaphoreType.DMA((2, count - 1)),
-            pltpu.SemaphoreType.DMA((2, count - 1)),
-        ],
-        compiler_params=pltpu.CompilerParams(
-            collective_id=0, has_side_effects=True, vmem_limit_bytes=VMEM_BYTES
-        ),
-        cost_estimate=pl.CostEstimate(
-            flops=0, bytes_accessed=30 * 1024 * 1024, transcendentals=0
-        ),
-        name="chain_gather",
-    )(block)
-
-
-def chain_scatter(count, part_ref, out_ref, held, sent, send_sem, recv_sem):
+    def middle(step):
+        arrive(step - 1)
+        start(step)
+
+    def last():
+        arrive(count - 2)
+        for step in range(count - 1):
+
+            @pl.when((me < count - 1) & (me - step >= 0))
+            def _():
+                hop(span(me - step), me - step, me + 1, 0, step).wait_send()
+
+            @pl.when((me > 0) & (me + step <= count - 1))
+            def _():
+                hop(span(me + step), me + step, me - 1, 1, step).wait_send()
+
+    return (
+        [functools.partial(start, 0)]
+        + [functools.partial(middle, step) for step in range(1, count - 1)]
+        + [last]
+    )
+
+
+def scatter_stages(count, part_ref, out_ref, held, sent, send_sem, recv_sem):
     me = lax.axis_index("col")
-    greet(me, count)
     rows = out_ref.shape[0]
 
     def mine(owner):
@@ -153,14 +158,17 @@
             send_sem=send_sem.at[way, owner],
             recv_sem=recv_sem.at[way, owner],
             device_id={"col": target},
-            device_id_type=pl.DeviceIdType.MESH,
-        )
-
-    for step in range(count - 1):
-        for way, owner, inside in (
+            device_id_type=MESH,
+        )
+
+    def flows(step):
+        return (
             (0, count - 1 - step, me < count - 1 - step),
             (1, step, me > step),
-        ):
+        )
+
+    def move(step):
+        for way, owner, inside in flows(step):
             first = me == 0 if way == 0 else me == count - 1
             target = me + 1 if way == 0 else me - 1
 
@@ -176,51 +184,331 @@
                 sent[way, owner] = total.astype(sent.dtype)
                 hop(way, owner, target).start()
 
-    out_ref[...] = mine(me)
-
-    @pl.when(me > 0)
-    def _():
-        hop(0, me, me).wait_recv()
-        out_ref[...] += held[0, me].astype(jnp.float32)
-
-    @pl.when(me < count - 1)
-    def _():
-        hop(1, me, me).wait_recv()
-        out_ref[...] += held[1, me].astype(jnp.float32)
-
-    for step in range(count - 1):
-        for way, owner, inside in (
-            (0, count - 1 - step, me < count - 1 - step),
-            (1, step, me > step),
-        ):
-
-            @pl.when(inside)
-            def _():
-                hop(way, owner, me).wait_send()
-
-
-def scatter_tokens(part):
-    count = lax.axis_size("col")
-    rows, width = part.shape[0] // count, part.shape[1]
-    return pl.pallas_call(
-        functools.partial(chain_scatter, count),
-        out_shape=jax.ShapeDtypeStruct((rows, width), jnp.float32),
-        in_specs=[pl.BlockSpec(memory_space=pltpu.VMEM)],
-        out_specs=pl.BlockSpec(memory_space=pltpu.VMEM),
-        scratch_shapes=[
-            pltpu.VMEM((2, count, rows, width), jnp.bfloat16),
-            pltpu.VMEM((2, count, rows, width), jnp.bfloat16),
-            pltpu.SemaphoreType.DMA((2, count)),
-            pltpu.SemaphoreType.DMA((2, count)),
-        ],
+    def last():
+        out_ref[...] = mine(me)
+
+        @pl.when(me > 0)
+        def _():
+            hop(0, me, me).wait_recv()
+            out_ref[...] += held[0, me].astype(jnp.float32)
+
+        @pl.when(me < count - 1)
+        def _():
+            hop(1, me, me).wait_recv()
+            out_ref[...] += held[1, me].astype(jnp.float32)
+
+        for step in range(count - 1):
+            for way, owner, inside in flows(step):
+
+                @pl.when(inside)
+                def _():
+                    hop(way, owner, me).wait_send()
+
+    return [functools.partial(move, step) for step in range(count - 1)] + [last]
+
+
+def weight_shape(part_shape, split):
+    rows, width = part_shape
+    return (rows // 2, width) if split == 0 else (rows, width // 2)
+
+
+def weight_scratch(part_shape, split, dp_count):
+    rows, width = weight_shape(part_shape, split)
+    count = len(reduce_levels(dp_count))
+    half = rows // 2
+    scratch = [
+        pltpu.VMEM((2, half, width), jnp.bfloat16),
+        pltpu.VMEM((half, width), jnp.bfloat16),
+        pltpu.VMEM((half, width), jnp.bfloat16),
+        pltpu.VMEM((half, width), jnp.float32),
+        pltpu.VMEM((rows, width), jnp.bfloat16),
+        pltpu.SemaphoreType.DMA((2 * count + 1,)),
+        pltpu.SemaphoreType.DMA((2 * count + 1,)),
+    ]
+    for level in range(2, count):
+        piece = half >> (level - 1)
+        scratch += [pltpu.VMEM((piece, width), jnp.bfloat16)] * 2
+    return scratch
+
+
+def weight_stages(split, dp_count, part_ref, out_ref, scratch):
+    near, toward, beside, total, whole, send_sem, recv_sem = scratch[:7]
+    deeper = scratch[7:]
+    levels = reduce_levels(dp_count)
+    rows, width = out_ref.shape
+    half = rows // 2
+    dp, row = lax.axis_index("dp"), lax.axis_index("row")
+
+    def at(side, start, size):
+        if split == 0:
+            return (pl.ds(pl.multiple_of(side * rows + start, size), size), slice(None))
+        return (
+            pl.ds(pl.multiple_of(start, size), size),
+            pl.ds(pl.multiple_of(side * width, width), width),
+        )
+
+    def copy(source, landing, place, level):
+        axis, bit = levels[level]
+        return pltpu.make_async_remote_copy(
+            src_ref=source,
+            dst_ref=landing,
+            send_sem=send_sem.at[place],
+            recv_sem=recv_sem.at[place],
+            device_id={axis: lax.axis_index(axis) ^ bit},
+            device_id_type=MESH,
+        )
+
+    low = dp % 2
+    core_copies = [
+        copy(part_ref.at[at(side, (1 - low) * half, half)], near.at[place], place, 0)
+        for place, side in ((0, 1 - row), (1, row))
+    ]
+    row_copy = copy(toward, beside, 2, 1)
+    waits = core_copies + [row_copy]
+    stages = []
+
+    def begin():
+        for item in core_copies:
+            item.start()
+
+    def summed(side, place):
+        return part_ref[at(side, low * half, half)].astype(jnp.float32) + near[place].astype(
+            jnp.float32
+        )
+
+    def core_done():
+        core_copies[0].wait_recv()
+        toward[...] = summed(1 - row, 0).astype(jnp.bfloat16)
+        row_copy.start()
+        core_copies[1].wait_recv()
+        total[...] = summed(row, 1)
+
+    kept, size = 0, half
+    halvings = []
+    for level in range(2, len(levels)):
+        side = (dp // levels[level][1]) % 2
+        size //= 2
+        item = copy(deeper[2 * level - 4], deeper[2 * level - 3], level + 1, level)
+        waits.append(item)
+        halvings.append((level, item, kept + (1 - side) * size, kept + side * size, size))
+        kept = kept + side * size
+
+    def send_halving(entry):
+        level, item, other, _, extent = entry
+        deeper[2 * level - 4][...] = total[
+            pl.ds(pl.multiple_of(other, extent), extent), :
+        ].astype(jnp.bfloat16)
+        item.start()
+
+    def take_halving(entry):
+        level, item, _, own, extent = entry
+        item.wait_recv()
+        place = pl.ds(pl.multiple_of(own, extent), extent)
+        total[place, :] = total[place, :] + deeper[2 * level - 3][...].astype(jnp.float32)
+
+    doublings = []
+    start, extent = low * half + kept, size
+    for level in list(range(len(levels) - 1, 1, -1)) + [0]:
+        place = len(levels) + 1 + len(doublings)
+        ref = whole.at[pl.ds(pl.multiple_of(start, extent), extent)]
+        side = (dp // levels[level][1]) % 2
+        item = copy(ref, ref, place, level)
+        other = whole.at[
+            pl.ds(pl.multiple_of(start + (1 - 2 * side) * extent, extent), extent)
+        ]
+        doublings.append((item, copy(other, other, place, level)))
+        start, extent = start - side * extent, 2 * extent
+
+    def start_doubling():
+        own = pl.ds(pl.multiple_of(low * half + kept, size), size)
+        whole[own, :] = total[pl.ds(pl.multiple_of(kept, size), size), :].astype(jnp.bfloat16)
+        doublings[0][0].start()
+
+    def row_done():
+        row_copy.wait_recv()
+        total[...] += beside[...].astype(jnp.float32)
+        if halvings:
+            send_halving(halvings[0])
+        else:
+            start_doubling()
+
+    def halved(position):
+        take_halving(halvings[position])
+        if position + 1 < len(halvings):
+            send_halving(halvings[position + 1])
+        else:
+            start_doubling()
+
+    def doubled(position):
+        doublings[position][1].wait_recv()
+        if position + 1 < len(doublings):
+            doublings[position + 1][0].start()
+        else:
+            out_ref[...] = whole[...].astype(jnp.float32)
+            for item in waits:
+                item.wait_send()
+            for item, _ in doublings:
+                item.wait_send()
+
+    stages = [begin, core_done, row_done]
+    stages += [functools.partial(halved, position) for position in range(len(halvings))]
+    stages += [functools.partial(doubled, position) for position in range(len(doublings))]
+    return stages
+
+
+def vector_stages(count, dp_count, shared, part_ref, out_ref, totals, landed, across, send_sem, recv_sem):
+    levels = reduce_levels(dp_count)
+    me = lax.axis_index("col")
+
+    def copy(level):
+        axis, bit = levels[level]
+        return pltpu.make_async_remote_copy(
+            src_ref=part_ref if level == 0 else totals.at[level - 1],
+            dst_ref=landed.at[level],
+            send_sem=send_sem.at[level],
+            recv_sem=recv_sem.at[level],
+            device_id={axis: lax.axis_index(axis) ^ bit},
+            device_id_type=MESH,
+        )
+
+    def spread(step):
+        return pltpu.make_async_remote_copy(
+            src_ref=totals.at[len(levels) - 1],
+            dst_ref=across.at[me],
+            send_sem=send_sem.at[len(levels) + step],
+            recv_sem=recv_sem.at[len(levels) + step],
+            device_id={"col": lax.rem(me + step, count)},
+            device_id_type=MESH,
+        )
+
+    def arrival(step):
+        return pltpu.make_async_remote_copy(
+            src_ref=totals.at[len(levels) - 1],
+            dst_ref=across.at[lax.rem(me - step + count, count)],
+            send_sem=send_sem.at[len(levels) + step],
+            recv_sem=recv_sem.at[len(levels) + step],
+            device_id={"col": lax.rem(me + step, count)},
+            device_id_type=MESH,
+        )
+
+    def take(level):
+        copy(level).wait_recv()
+        held = part_ref[...] if level == 0 else totals[level - 1]
+        totals[level] = held + landed[level]
+        if level + 1 < len(levels):
+            copy(level + 1).start()
+        else:
+            across[me] = totals[level]
+            for step in range(1, count):
+                spread(step).start()
+
+    def finish():
+        for step in range(1, count):
+            arrival(step).wait_recv()
+        whole = across[0]
+        for other in range(1, count):
+            whole = whole + across[other]
+        shared_rows = lax.broadcasted_iota(jnp.int32, whole.shape, 0) < shared
+        out_ref[...] = jnp.where(shared_rows, whole, totals[len(levels) - 1])
+        for level in range(len(levels)):
+            copy(level).wait_send()
+        for step in range(1, count):
+            spread(step).wait_send()
+
+    return (
+        [lambda: copy(0).start()]
+        + [functools.partial(take, level) for level in range(len(levels))]
+        + [finish]
+    )
+
+
+def chain_kernel(kind, split, shared, count, dp_count, sizes, *refs):
+    me = lax.axis_index("col")
+    refs = list(refs)
+
+    def pull(number):
+        taken = refs[:number]
+        del refs[:number]
+        return taken
+
+    extras = (split is not None) + (shared > 0)
+    inputs, outputs = pull(1 + extras), pull(1 + extras)
+    greet(me, count, reduce_levels(dp_count) if extras else [], shared > 0)
+    chain = (gather_stages if kind == "gather" else scatter_stages)(
+        count, inputs[0], outputs[0], *pull(sizes[0])
+    )
+    weight, vector = [], []
+    if split is not None:
+        weight = weight_stages(split, dp_count, inputs[1], outputs[1], pull(sizes[1]))
+    if shared > 0:
+        vector = vector_stages(count, dp_count, shared, inputs[2], outputs[2], *pull(sizes[2]))
+    order = []
+    for position in range(max(len(chain), len(weight), len(vector))):
+        if position < len(chain):
+            order.append(chain[position])
+        if position < len(vector):
+            order.append(vector[position])
+        if position < len(weight):
+            order.append(weight[position])
+    for stage in order:
+        stage()
+
+
+def chain_call(kind, ident, block, weight=None, split=None, vectors=None, shared=0):
+    count, dp_count = lax.axis_size("col"), lax.axis_size("dp")
+    rows, width = block.shape
+    operands, sizes = [block], [0, 0, 0]
+    if kind == "gather":
+        shapes = [jax.ShapeDtypeStruct((count * rows, width), block.dtype)]
+        scratch = [pltpu.SemaphoreType.DMA((2, count - 1))] * 2
+    else:
+        rows //= count
+        shapes = [jax.ShapeDtypeStruct((rows, width), jnp.float32)]
+        scratch = [pltpu.VMEM((2, count, rows, width), jnp.bfloat16)] * 2
+        scratch += [pltpu.SemaphoreType.DMA((2, count))] * 2
+    sizes[0] = len(scratch)
+    if weight is not None:
+        operands.append(weight)
+        shapes.append(jax.ShapeDtypeStruct(weight_shape(weight.shape, split), jnp.float32))
+        more = weight_scratch(weight.shape, split, dp_count)
+        sizes[1] = len(more)
+        scratch += more
+    if vectors is not None:
+        operands.append(vectors)
+        shapes.append(jax.ShapeDtypeStruct(vectors.shape, vectors.dtype))
+        levels = len(reduce_levels(dp_count))
+        more = [
+            pltpu.VMEM((levels,) + vectors.shape, vectors.dtype),
+            pltpu.VMEM((levels,) + vectors.shape, vectors.dtype),
+            pltpu.VMEM((count,) + vectors.shape, vectors.dtype),
+            pltpu.SemaphoreType.DMA((levels + count,)),
+            pltpu.SemaphoreType.DMA((levels + count,)),
+        ]
+        sizes[2] = len(more)
+        scratch += more
+    results = pl.pallas_call(
+        functools.partial(chain_kernel, kind, split, shared, count, dp_count, tuple(sizes)),
+        out_shape=shapes,
+        in_specs=[pl.BlockSpec(memory_space=pltpu.VMEM)] * len(operands),
+        out_specs=[pl.BlockSpec(memory_space=pltpu.VMEM)] * len(operands),
+        scratch_shapes=scratch,
         compiler_params=pltpu.CompilerParams(
-            collective_id=1, has_side_effects=True, vmem_limit_bytes=VMEM_BYTES
+            collective_id=ident, has_side_effects=True, vmem_limit_bytes=VMEM_BYTES
         ),
         cost_estimate=pl.CostEstimate(
-            flops=0, bytes_accessed=30 * 1024 * 1024, transcendentals=0
+            flops=0, bytes_accessed=60 * 1024 * 1024, transcendentals=0
         ),
-        name="chain_scatter",
-    )(part)
+        name="chain_" + kind + str(ident),
+    )(*operands)
+    return results[0] if len(results) == 1 else results
+
+
+def gather_tokens(block):
+    return chain_call("gather", 0, block)
+
+
+def scatter_tokens(part):
+    return chain_call("scatter", 1, part)
 
 
 def slot_moves(swap):
@@ -396,18 +684,21 @@
     grad_narrowed = grad_second.astype(jnp.bfloat16)
     narrow_bias_part = jnp.sum(grad_narrowed, axis=0, dtype=jnp.float32)
     grad_narrow_block = gather_tokens(grad_narrowed)
-    narrow_total = weight_total(inner_rows(active_block, grad_narrow_block), 1)
+    narrow_part = inner_rows(active_block, grad_narrow_block).astype(jnp.bfloat16)
     grad_active = outer_back(grad_narrow_block, narrow_weight)
     grad_widened = gelu_pull(grad_active)[0].astype(jnp.bfloat16)
     widen_bias_part = jnp.sum(grad_widened, axis=0, dtype=jnp.float32)
-    grad_first = scatter_tokens(outer_back(grad_widened, widen_weight)) + grad_second
-    widen_total = weight_total(inner_rows(gathered_first, grad_widened), 0)
+    grad_first, narrow_total = chain_call(
+        "scatter", 2, outer_back(grad_widened, widen_weight), narrow_part, 1
+    )
+    grad_first = grad_first + grad_second
+    widen_part = inner_rows(gathered_first, grad_widened).astype(jnp.bfloat16)
     first_gain_part = jnp.sum(grad_first * first_normal, axis=0)
     first_shift_part = jnp.sum(grad_first, axis=0)
     grad_attended = norm_backward(grad_first, first_normal, first_inverse, first_gain)
     grad_mix = grad_attended.astype(jnp.bfloat16)
     mixer_bias_part = jnp.sum(grad_mix, axis=0, dtype=jnp.float32)
-    grad_mixer_block = gather_tokens(grad_mix)
+    grad_mixer_block, widen_total = chain_call("gather", 3, grad_mix, widen_part, 0)
     mixer_total = weight_total(inner_rows(mixed_block, grad_mixer_block), 1)
     grad_mixed = outer_back(grad_mixer_block, mixer_weight).astype(jnp.bfloat16)
     grad_heads = grad_mixed.reshape(slot_rows, heads_here, HD)
@@ -415,10 +706,9 @@
     grad_packed = grad_slots.reshape(slot_rows, heads_here * 3 * HD).astype(jnp.bfloat16)
     packed_sums = jnp.sum(grad_packed, axis=0, dtype=jnp.float32).reshape(heads_here, 3, HD)
     attend_bias_part = jnp.concatenate([packed_sums[:, 0], packed_sums[:, 2]], axis=1)
-    attend_total = weight_total(inner_rows(gathered_input, grad_packed), 0)
-    input_gradient = scatter_tokens(outer_back(grad_packed, attend_weight)) + grad_attended
-    input_gradient = from_slot_rows(input_gradient)
-    column_totals = lax.psum((attend_bias_part, widen_bias_part), ("dp", "row"))
+    attend_part = inner_rows(gathered_input, grad_packed).astype(jnp.bfloat16)
+    model = mixer_bias_part.shape[0]
+    attend_bias_flat = attend_bias_part.reshape(-1)
     vector_parts = jnp.stack(
         [
             mixer_bias_part,
@@ -427,11 +717,19 @@
             narrow_bias_part,
             second_gain_part,
             second_shift_part,
+            jnp.pad(widen_bias_part, (0, model - widen_bias_part.shape[0])),
+            jnp.pad(attend_bias_flat, (0, model - attend_bias_flat.shape[0])),
         ]
     )
-    half = vector_parts.shape[1] // 2
-    vector_totals = lax.dynamic_slice_in_dim(
-        lax.psum(vector_parts, ("dp", "row", "col")), row_rank * half, half, 1
+    input_gradient, attend_total, vector_sums = chain_call(
+        "scatter", 4, outer_back(grad_packed, attend_weight), attend_part, 0, vector_parts, 6
+    )
+    input_gradient = from_slot_rows(input_gradient + grad_attended)
+    half = model // 2
+    vector_totals = lax.dynamic_slice_in_dim(vector_sums, row_rank * half, half, 1)
+    column_totals = (
+        vector_sums[7, : attend_bias_flat.shape[0]].reshape(attend_bias_part.shape),
+        vector_sums[6, : widen_bias_part.shape[0]],
     )
     return (
         layer_output,

time: 451 us -> 408 us (0.905)
  Pallas kernels: 177 us -> 249 us
  waiting for transfers between devices: 92.8 us -> 35.2 us
  blocking collectives: 73.5 us -> 19.2 us
  starting transfers between devices: 26.7 us -> 17.5 us
  local copies, waits for them, and re-layouts: 9.41 us -> 16.6 us
    reduce_scatter x4 -> x1, waiting for transfers between devices: 91.2 us -> 0.01 us  [weight_total(): lax.psum_scatter(part.astype(jnp.bfloat16), 'row', scatter_dimension=dime...]
    pallas_call x8, Pallas kernels: 177 us -> 249 us  [chain_call(): pl.pallas_call(functools.partial(chain_kernel, kind, split, shared, count...]
    psum x2 -> x0, blocking collectives: 54.3 us -> none  [the longest x1 40 us: per_device(): lax.psum(vector_parts, ('dp', 'row', 'col'))]
    ppermute x4, waiting for transfers between devices: 0.01 us -> 22.1 us  [from_slot_rows(): landed.append(lax.ppermute(piece, ('row', 'col'), pairs))]
    psum x1, waiting for transfers between devices: 0.01 us -> 11.6 us  [weight_total(): return lax.psum(part, 'dp').astype(jnp.float32)]
    ppermute x4, starting transfers between devices: 15.2 us -> 6.37 us  [from_slot_rows(): landed.append(lax.ppermute(piece, ('row', 'col'), pairs))]
    unnamed x66 -> x81, local copies, waits for them, and re-layouts: 5.24 us -> 11.1 us
    convert_element_type x4 -> x1, other arithmetic: 7.45 us -> 1.95 us  [weight_total(): return lax.psum(part, 'dp').astype(jnp.float32)]
  transfers between devices with their start and end apart: 16 -> 13, of which waited for: 3 -> 3; matrix products, arithmetic and copies ran while one was open for 9% -> 7% of each run, Pallas kernels for 20% -> 27%
where the time goes in v2:
time: 408 us; the launch traced here: 406 us
  Pallas kernels  249 us (61%)
  matrix products  40.3 us (10%)
  waiting for transfers between devices  35.2 us (9%)
  blocking collectives  19.2 us (5%)
  starting transfers between devices  17.5 us (4%)
  local copies, waits for them, and re-layouts  16.6 us (4%)
  between operations  14.6 us (4%)
  other arithmetic  13.8 us (3%)
    pallas_call x8, Pallas kernels, chain_call(): pl.pallas_call(functools.partial(chain_kernel, kind, split, shared, count...  249 us
    ppermute x4, waiting for transfers between devices, from_slot_rows(): landed.append(lax.ppermute(piece, ('row', 'col'), pairs))  22.1 us
    dot_general x4, matrix products, product(): return jnp.dot(left_side, right_side, preferred_element_type=jnp.float32)  15.7 us
    all_gather x1, blocking collectives, per_device(): mixer_weight = lax.all_gather(mixer_weight, 'row', axis=1, tiled=True)  14.4 us
    psum x1, waiting for transfers between devices, weight_total(): return lax.psum(part, 'dp').astype(jnp.float32)  11.6 us
    unnamed x81, local copies, waits for them, and re-layouts  11.1 us
    ppermute x4, starting transfers between devices, to_slot_rows(): landed.append(lax.ppermute(block, ('row', 'col'), slot_moves(swap)))  10.9 us
  transfers between devices with their start and end apart: 13, of which 3 were waited for; matrix products, arithmetic and copies ran while one was open for 7% of the time, Pallas kernels for 27%

profile of v2, /device:TPU:8, one launch (start us, length us, event | category | flops | bytes accessed | tf_op | source)
XLA Modules:
  0.0 406.2 jit_solution(17660354530808127813)
XLA Ops:
  9.8 2.6 collective-permute-start
  12.5 2.3 collective-permute-start.1
  16.2 4.6 %collective-permute-start.5 = (bf16[128,512]{1,0:T(8,128)(2,1)S(1)}, bf16[128,512]{1,0:T(8,128)(2,1)S(1)}, u32[]{:S(2)}, u32[]{:S(2)}) collective-permute-start(bf16[128,512]{1,0:T(8,128)(2,1)S(1)} %get-tuple-element.61), channel_id=1, source_target_pairs={{0,0},{1,2},{2,4},{3,6},{4,1},{5,3},{6,5},{7,7},{8,8},{9,10},{10,1... | collective-permute-start | bytes 393224 | tf_op jit(solution)/shard_map/ppermute | solution.py:531
  23.1 4.7 %all_gather.17 = f32[6,1024]{1,0:T(8,128)S(1)} all-gather(f32[6,512]{1,0:T(8,128)S(1)} %stack.66), channel_id=1, replica_groups=mesh['dp'=4,'row'=2,'col'=4] {'row'}, dimensions={1}, use_global_device_ids=true | all-gather | bytes 36864 | tf_op jit(solution)/shard_map/all_gather | solution.py:644
  27.9 14.4 %all_gather.16 = bf16[256,1024]{1,0:T(8,128)(2,1)S(1)} all-gather(bf16[256,512]{1,0:T(8,128)(2,1)S(1)} %copy-done.20), channel_id=1, replica_groups=mesh['dp'=4,'row'=2,'col'=4] {'row'}, dimensions={1}, use_global_device_ids=true | all-gather | bytes 786432 | tf_op jit(solution)/shard_map/all_gather | solution.py:647
  42.4 17.7 %chain_gather0.3 = bf16[512,1024]{1,0:T(8,128)(2,1)S(1)} custom-call(bf16[128,1024]{1,0:T(8,128)(2,1)S(1)} %pad_maximum_fusion.1.refs_0_), custom_call_target="tpu_custom_call" | custom-call | bytes 62914560 | tf_op jit(solution)/shard_map/chain_gather0/pallas_call | solution.py:489
  60.3 3.3 add_convert_fusion.1
  69.9 26.7 %chain_scatter1.2 = f32[128,1024]{1,0:T(8,128)S(1)} custom-call(f32[512,1024]{1,0:T(8,128)S(1)} %fusion.30.refs_0_), custom_call_target="tpu_custom_call" | custom-call | bytes 62914560 | tf_op jit(solution)/shard_map/chain_scatter1/pallas_call | solution.py:489
  97.2 17.3 %chain_gather0.4 = bf16[512,1024]{1,0:T(8,128)(2,1)S(1)} custom-call(bf16[128,1024]{1,0:T(8,128)(2,1)S(1)} %fusion.21.refs_0_), custom_call_target="tpu_custom_call" | custom-call | bytes 62914560 | tf_op jit(solution)/shard_map/chain_gather0/pallas_call | solution.py:489
  114.6 8.7 %multiply_convert_fusion.1 = (bf16[512,1024]{1,0:T(8,128)(2,1)}, f32[512,1024]{1,0:T(8,128)}, f32[512,1024]{1,0:T(8,128)}) fusion(f32[1024]{0:T(1024)S(1)} %copy-done.34, bf16[512,1024]{1,0:T(8,128)(2,1)S(1)} %chain_gather0.4, bf16[1024,1024]{1,0:T(8,128)(2,1)} %all-gather.6.cloned.1.call-done), kind=kOutput, calls=%fused_computation.14 | convolution fusion | flops 1108344832 | bytes 8392704 | tf_op jit(solution)/shard_map/dot_general | solution.py:19
  123.3 3.2 fusion.31.refs_0_
  126.5 28.2 %chain_scatter1.3 = f32[128,1024]{1,0:T(8,128)S(1)} custom-call(f32[512,1024]{1,0:T(8,128)S(1)} %fusion.31.refs_0_), custom_call_target="tpu_custom_call" | custom-call | bytes 62914560 | tf_op jit(solution)/shard_map/chain_scatter1/pallas_call | solution.py:489
  156.6 16.0 %chain_gather0.5 = bf16[512,1024]{1,0:T(8,128)(2,1)S(1)} custom-call(bf16[128,1024]{1,0:T(8,128)(2,1)S(1)} %get-tuple-element.41.refs_0_), custom_call_target="tpu_custom_call" | custom-call | bytes 62914560 | tf_op jit(solution)/shard_map/chain_gather0/pallas_call | solution.py:489
  172.7 2.7 convolution_convert_fusion.1.refs_1_
  176.2 2.5 convert_reduce_fusion
  181.7 53.7 %chain_scatter2.1 = (f32[128,1024]{1,0:T(8,128)S(1)}, f32[1024,512]{1,0:T(8,128)S(1)}) custom-call(f32[512,1024]{1,0:T(8,128)S(1)} %fusion.32.refs_0_, bf16[1024,1024]{1,0:T(8,128)(2,1)} %convolution_convert_fusion.1.refs_1_), custom_call_target="tpu_custom_call" | custom-call | bytes 62914560 | tf_op jit(solution)/shard_map/chain_scatter2/pallas_call | solution.py:489
  236.2 1.6 convert_reduce_fusion.3
  237.8 39.6 %chain_gather3.1 = (bf16[512,1024]{1,0:T(8,128)(2,1)S(1)}, f32[512,1024]{1,0:T(8,128)S(1)}) custom-call(bf16[128,1024]{1,0:T(8,128)(2,1)S(1)} %get-tuple-element.44.refs_0_, bf16[1024,1024]{1,0:T(8,128)(2,1)S(1)} %convolution_convert_fusion.refs_1_), custom_call_target="tpu_custom_call" | custom-call | bytes 62914560 | tf_op jit(solution)/shard_map/chain_gather3/pallas_call | solution.py:489
  280.5 3.8 fusion.12
  284.3 1.9 multiply_reduce_fusion
  287.4 1.5 fusion.15
  290.7 1.6 collective-permute-start.2
  292.4 2.8 collective-permute-start.3
  296.6 2.2 convolution_convert_fusion.2.refs_1_
  298.9 2.8 fusion.33.refs_0_
  301.8 49.8 %chain_scatter4.1 = (f32[128,1024]{1,0:T(8,128)S(1)}, f32[512,768]{1,0:T(8,128)S(1)}, f32[8,1024]{1,0:T(8,128)S(1)}) custom-call(f32[512,1024]{1,0:T(8,128)S(1)} %fusion.33.refs_0_, bf16[1024,768]{1,0:T(8,128)(2,1)S(1)} %copy-done.2, f32[8,1024]{1,0:T(8,128)S(1)} %stack.79.refs_2_), custom_call_target="tpu_custom_call" | custom-call | bytes 62914560 | tf_op jit(solution)/shard_map/chain_scatter4/pallas_call | solution.py:489
  353.5 1.9 collective-permute-start.7
  357.8 5.8 %collective-permute-done.6 = f32[128,512]{1,0:T(8,128)S(1)} collective-permute-done((f32[128,512]{1,0:T(8,128)S(1)}, f32[128,512]{1,0:T(8,128)S(1)}, u32[]{:S(2)}, u32[]{:S(2)}) %collective-permute-start.6) | collective-permute-done | bytes 262176 | tf_op jit(solution)/shard_map/ppermute | solution.py:545
  363.6 16.3 %collective-permute-done.7 = f32[128,512]{1,0:T(8,128)S(1)} collective-permute-done((f32[128,512]{1,0:T(8,128)S(1)}, f32[128,512]{1,0:T(8,128)S(1)}, u32[]{:S(2)}, u32[]{:S(2)}) %collective-permute-start.7) | collective-permute-done | bytes 262176 | tf_op jit(solution)/shard_map/ppermute | solution.py:545
  380.8 11.6 %all-reduce.3.cloned.1.call-done = bf16[256,512]{1,0:T(8,128)(2,1)} async-done(((bf16[256,512]{1,0:T(8,128)(2,1)}), bf16[256,512]{1,0:T(8,128)(2,1)}) %all-reduce.3.cloned.1.call-update) | async-done | bytes 262160 | tf_op jit(solution)/shard_map/psum | solution.py:615
  392.5 2.0 convert_element_type.107
  394.4 2.7 copy.67
  (159 shorter events, 35.1 us)
Async XLA Ops:
  7.2 13.7 %copy-start.35 = (s32[2]{0:T(128)S(1)}, s32[2]{0:T(128)}, u32[]{:S(2)}) copy-start(s32[2]{0:T(128)} %param.16) | copy-start | bytes 28
  7.2 15.6 %copy-start.24 = (f32[4,128]{1,0:T(4,128)S(1)}, f32[4,128]{1,0:T(4,128)}, u32[]{:S(2)}) copy-start(f32[4,128]{1,0:T(4,128)} %param.18) | copy-start | bytes 6148
  7.2 15.9 %copy-start.31 = (f32[512]{0:T(512)S(1)}, f32[512]{0:T(512)}, u32[]{:S(2)}) copy-start(f32[512]{0:T(512)} %param.28) | copy-start | bytes 6148
  7.2 15.9 %copy-start.30 = (f32[512]{0:T(512)S(1)}, f32[512]{0:T(512)}, u32[]{:S(2)}) copy-start(f32[512]{0:T(512)} %param.27) | copy-start | bytes 6148
  7.2 15.8 %copy-start.29 = (f32[512]{0:T(512)S(1)}, f32[512]{0:T(512)}, u32[]{:S(2)}) copy-start(f32[512]{0:T(512)} %param.26) | copy-start | bytes 6148
  7.2 15.8 %copy-start.28 = (f32[512]{0:T(512)S(1)}, f32[512]{0:T(512)}, u32[]{:S(2)}) copy-start(f32[512]{0:T(512)} %param.22) | copy-start | bytes 6148
  7.3 15.8 %copy-start.27 = (f32[512]{0:T(512)S(1)}, f32[512]{0:T(512)}, u32[]{:S(2)}) copy-start(f32[512]{0:T(512)} %param.21) | copy-start | bytes 6148
  7.3 15.8 %copy-start.26 = (f32[512]{0:T(512)S(1)}, f32[512]{0:T(512)}, u32[]{:S(2)}) copy-start(f32[512]{0:T(512)} %param.20) | copy-start | bytes 6148
  7.3 20.6 %copy-start.20 = (bf16[256,512]{1,0:T(8,128)(2,1)S(1)}, bf16[256,512]{1,0:T(8,128)(2,1)}, u32[]{:S(2)}) copy-start(bf16[256,512]{1,0:T(8,128)(2,1)} %param.19) | copy-start | bytes 786436
  7.3 53.0 %all-gather.4.cloned.1.call-start = ((), (), s32[]{:S(2)}) async-start(), calls=%async_computation.1 | async-start | bytes 2359296 | tf_op jit(solution)/shard_map/all_gather | solution.py:646
  8.0 106.5 %all-gather.6.cloned.1.call-start = ((), (), s32[]{:S(2)}) async-start(), calls=%async_computation.2 | async-start | bytes 3145728 | tf_op jit(solution)/shard_map/all_gather | solution.py:648
  8.8 114.6 %all-gather.8.cloned.1.call-start = ((), (), s32[]{:S(2)}) async-start(), calls=%async_computation.3 | async-start | bytes 3145728 | tf_op jit(solution)/shard_map/all_gather | solution.py:649
  9.8 32.5 %collective-permute-start = (bf16[128,512]{1,0:T(8,128)(2,1)S(1)}, bf16[128,512]{1,0:T(8,128)(2,1)S(1)}, u32[]{:S(2)}, u32[]{:S(2)}) collective-permute-start(bf16[128,512]{1,0:T(8,128)(2,1)S(1)} %get-tuple-element.68), channel_id=1, source_target_pairs={{0,1},{1,3},{2,5},{3,7},{4,0},{5,2},{6,4},{7,6},{8,9},{9,11},{10,1... | collective-permute-start | bytes 393224 | tf_op jit(solution)/shard_map/ppermute | solution.py:531
  12.5 29.9 %collective-permute-start.1 = (bf16[128,512]{1,0:T(8,128)(2,1)S(1)}, bf16[128,512]{1,0:T(8,128)(2,1)S(1)}, u32[]{:S(2)}, u32[]{:S(2)}) collective-permute-start(bf16[128,512]{1,0:T(8,128)(2,1)S(1)} %get-tuple-element.69), channel_id=1, source_target_pairs={{0,0},{1,2},{2,4},{3,6},{4,1},{5,3},{6,5},{7,7},{8,8},{9,10},{10,1... | collective-permute-start | bytes 393224 | tf_op jit(solution)/shard_map/ppermute | solution.py:531
  14.8 45.4 %collective-permute-start.4 = (bf16[128,512]{1,0:T(8,128)(2,1)S(1)}, bf16[128,512]{1,0:T(8,128)(2,1)S(1)}, u32[]{:S(2)}, u32[]{:S(2)}) collective-permute-start(bf16[128,512]{1,0:T(8,128)(2,1)S(1)} %get-tuple-element.60), channel_id=1, source_target_pairs={{0,1},{1,3},{2,5},{3,7},{4,0},{5,2},{6,4},{7,6},{8,9},{9,11},{10,1... | collective-permute-start | bytes 393224 | tf_op jit(solution)/shard_map/ppermute | solution.py:531
  16.2 44.0 %collective-permute-start.5 = (bf16[128,512]{1,0:T(8,128)(2,1)S(1)}, bf16[128,512]{1,0:T(8,128)(2,1)S(1)}, u32[]{:S(2)}, u32[]{:S(2)}) collective-permute-start(bf16[128,512]{1,0:T(8,128)(2,1)S(1)} %get-tuple-element.61), channel_id=1, source_target_pairs={{0,0},{1,2},{2,4},{3,6},{4,1},{5,3},{6,5},{7,7},{8,8},{9,10},{10,1... | collective-permute-start | bytes 393224 | tf_op jit(solution)/shard_map/ppermute | solution.py:531
  20.8 337.0 %reduce-scatter.2.cloned.1.call-start = ((), (), s32[]{:S(2)}) async-start(), calls=%async_computation.4 | async-start | bytes 786432 | tf_op jit(solution)/shard_map/reduce_scatter | solution.py:612
  42.4 26.4 %copy-start.11 = (bf16[256,1024]{1,0:T(8,128)(2,1)}, bf16[256,1024]{1,0:T(8,128)(2,1)S(1)}, u32[]{:S(2)}) copy-start(bf16[256,1024]{1,0:T(8,128)(2,1)S(1)} %all_gather.16) | copy-start | bytes 1572868
  42.4 21.1 %copy-start.13 = (bf16[128,512]{1,0:T(8,128)(2,1)}, bf16[128,512]{1,0:T(8,128)(2,1)S(1)}, u32[]{:S(2)}) copy-start(bf16[128,512]{1,0:T(8,128)(2,1)S(1)} %get-tuple-element.67) | copy-start | bytes 393220
  69.5 27.2 %copy-start.14 = (bf16[128,512]{1,0:T(8,128)(2,1)S(1)}, bf16[128,512]{1,0:T(8,128)(2,1)}, u32[]{:S(2)}) copy-start(bf16[128,512]{1,0:T(8,128)(2,1)} %copy-done.13) | copy-start | bytes 393220
  96.6 18.0 %copy-start.34 = (f32[1024]{0:T(1024)S(1)}, f32[1024]{0:T(1024)}, u32[]{:S(2)}) copy-start(f32[1024]{0:T(1024)} %param.24) | copy-start | bytes 12292
  96.8 57.9 %copy-start.6 = (f32[128,1024]{1,0:T(8,128)}, f32[128,1024]{1,0:T(8,128)S(1)}, u32[]{:S(2)}) copy-start(f32[128,1024]{1,0:T(8,128)S(1)} %get-tuple-element.52) | copy-start | bytes 1572868
  155.2 17.4 %copy-start.36 = (bf16[512,1024]{1,0:T(8,128)(2,1)S(1)}, bf16[512,1024]{1,0:T(8,128)(2,1)}, u32[]{:S(2)}) copy-start(bf16[512,1024]{1,0:T(8,128)(2,1)} %get-tuple-element.49) | copy-start | bytes 3145732
  181.7 53.7 %copy-start.7 = (f32[128,1024]{1,0:T(8,128)S(1)}, f32[128,1024]{1,0:T(8,128)}, u32[]{:S(2)}) copy-start(f32[128,1024]{1,0:T(8,128)} %copy-done.6) | copy-start | bytes 1572868
  236.2 42.5 %copy-start.12 = (bf16[256,1024]{1,0:T(8,128)(2,1)S(1)}, bf16[256,1024]{1,0:T(8,128)(2,1)}, u32[]{:S(2)}) copy-start(bf16[256,1024]{1,0:T(8,128)(2,1)} %copy-done.11) | copy-start | bytes 1572868
  237.8 41.4 %copy-start.18 = (bf16[4,64,512]{2,1,0:T(8,128)(2,1)S(1)}, bf16[4,64,512]{2,1,0:T(8,128)(2,1)}, u32[]{:S(2)}) copy-start(bf16[4,64,512]{2,1,0:T(8,128)(2,1)} %copy-done.17) | copy-start | bytes 786436
  290.7 65.4 %collective-permute-start.2 = (bf16[128,512]{1,0:T(8,128)(2,1)}, bf16[128,512]{1,0:T(8,128)(2,1)S(1)}, u32[]{:S(2)}, u32[]{:S(2)}) collective-permute-start(bf16[128,512]{1,0:T(8,128)(2,1)} %get-tuple-element.64), channel_id=1, source_target_pairs={{1,0},{3,1},{5,2},{7,3},{0,4},{2,5},{4,6},{6,7},{9,8},{11,9},{13,1... | collective-permute-start | bytes 393224 | tf_op jit(solution)/shard_map/ppermute | solution.py:545
  292.4 63.8 %collective-permute-start.3 = (bf16[128,512]{1,0:T(8,128)(2,1)}, bf16[128,512]{1,0:T(8,128)(2,1)}, u32[]{:S(2)}, u32[]{:S(2)}) collective-permute-start(bf16[128,512]{1,0:T(8,128)(2,1)} %get-tuple-element.65), channel_id=1, source_target_pairs={{0,0},{2,1},{4,2},{6,3},{1,4},{3,5},{5,6},{7,7},{8,8},{10,9},{12,1... | collective-permute-start | bytes 393224 | tf_op jit(solution)/shard_map/ppermute | solution.py:545
  295.2 97.3 %all-reduce.3.cloned.1.call-start = ((), (), s32[]{:S(2)}) async-start(), calls=%async_computation.5 | async-start | bytes 524288 | tf_op jit(solution)/shard_map/psum | solution.py:615
  301.8 51.6 %copy-start.10 = (f32[128,1024]{1,0:T(8,128)S(1)}, f32[128,1024]{1,0:T(8,128)}, u32[]{:S(2)}) copy-start(f32[128,1024]{1,0:T(8,128)} %get-tuple-element.45) | copy-start | bytes 1572868
  353.5 10.2 %collective-permute-start.6 = (f32[128,512]{1,0:T(8,128)S(1)}, f32[128,512]{1,0:T(8,128)S(1)}, u32[]{:S(2)}, u32[]{:S(2)}) collective-permute-start(f32[128,512]{1,0:T(8,128)S(1)} %get-tuple-element.56), channel_id=1, source_target_pairs={{1,0},{3,1},{5,2},{7,3},{0,4},{2,5},{4,6},{6,7},{9,8},{11,9},{13,1... | collective-permute-start | bytes 786440 | tf_op jit(solution)/shard_map/ppermute | solution.py:545
  353.5 26.4 %collective-permute-start.7 = (f32[128,512]{1,0:T(8,128)S(1)}, f32[128,512]{1,0:T(8,128)S(1)}, u32[]{:S(2)}, u32[]{:S(2)}) collective-permute-start(f32[128,512]{1,0:T(8,128)S(1)} %get-tuple-element.57), channel_id=1, source_target_pairs={{0,0},{2,1},{4,2},{6,3},{1,4},{3,5},{5,6},{7,7},{8,8},{10,9},{12,1... | collective-permute-start | bytes 786440 | tf_op jit(solution)/shard_map/ppermute | solution.py:545
  (20 other events, 55.6 us)
Sparse Core Ops, SparseCore 0:
  9.7 36.8 all-gather.3
  48.1 33.8 all-gather.5
  83.5 33.1 all-gather.7
  295.3 14.6 reduce-scatter.1
  358.0 34.4 all-reduce.2

commit v3 on v2

--- a/solution.py
+++ b/solution.py
@@ -37,6 +37,7 @@
 
 VMEM_BYTES = 48 * 1024 * 1024
 MESH = pl.DeviceIdType.MESH
+CHUNKS = 2
 
 
 def reduce_levels(dp_count):
@@ -146,17 +147,18 @@
 
 def scatter_stages(count, part_ref, out_ref, held, sent, send_sem, recv_sem):
     me = lax.axis_index("col")
-    rows = out_ref.shape[0]
-
-    def mine(owner):
-        return part_ref[pl.ds(pl.multiple_of(owner * rows, rows), rows), :].astype(jnp.float32)
-
-    def hop(way, owner, target):
+    rows = out_ref.shape[0] // CHUNKS
+
+    def mine(owner, chunk):
+        start = pl.multiple_of((owner * CHUNKS + chunk) * rows, rows)
+        return part_ref[pl.ds(start, rows), :].astype(jnp.float32)
+
+    def hop(way, owner, chunk, target):
         return pltpu.make_async_remote_copy(
-            src_ref=sent.at[way, owner],
-            dst_ref=held.at[way, owner],
-            send_sem=send_sem.at[way, owner],
-            recv_sem=recv_sem.at[way, owner],
+            src_ref=sent.at[way, owner, chunk],
+            dst_ref=held.at[way, owner, chunk],
+            send_sem=send_sem.at[way, owner, chunk],
+            recv_sem=recv_sem.at[way, owner, chunk],
             device_id={"col": target},
             device_id_type=MESH,
         )
@@ -167,42 +169,49 @@
             (1, step, me > step),
         )
 
+    def one(way, owner, inside, chunk):
+        first = me == 0 if way == 0 else me == count - 1
+        target = me + 1 if way == 0 else me - 1
+
+        @pl.when(inside & first)
+        def _():
+            sent[way, owner, chunk] = mine(owner, chunk).astype(sent.dtype)
+            hop(way, owner, chunk, target).start()
+
+        @pl.when(inside & jnp.logical_not(first))
+        def _():
+            hop(way, owner, chunk, target).wait_recv()
+            total = mine(owner, chunk) + held[way, owner, chunk].astype(jnp.float32)
+            sent[way, owner, chunk] = total.astype(sent.dtype)
+            hop(way, owner, chunk, target).start()
+
     def move(step):
-        for way, owner, inside in flows(step):
-            first = me == 0 if way == 0 else me == count - 1
-            target = me + 1 if way == 0 else me - 1
-
-            @pl.when(inside & first)
+        for chunk in range(CHUNKS):
+            for way, owner, inside in flows(step):
+                one(way, owner, inside, chunk)
+
+    def last():
+        for chunk in range(CHUNKS):
+            place = pl.ds(chunk * rows, rows)
+            out_ref[place, :] = mine(me, chunk)
+
+            @pl.when(me > 0)
             def _():
-                sent[way, owner] = mine(owner).astype(sent.dtype)
-                hop(way, owner, target).start()
-
-            @pl.when(inside & jnp.logical_not(first))
+                hop(0, me, chunk, me).wait_recv()
+                out_ref[place, :] += held[0, me, chunk].astype(jnp.float32)
+
+            @pl.when(me < count - 1)
             def _():
-                hop(way, owner, target).wait_recv()
-                total = mine(owner) + held[way, owner].astype(jnp.float32)
-                sent[way, owner] = total.astype(sent.dtype)
-                hop(way, owner, target).start()
-
-    def last():
-        out_ref[...] = mine(me)
-
-        @pl.when(me > 0)
-        def _():
-            hop(0, me, me).wait_recv()
-            out_ref[...] += held[0, me].astype(jnp.float32)
-
-        @pl.when(me < count - 1)
-        def _():
-            hop(1, me, me).wait_recv()
-            out_ref[...] += held[1, me].astype(jnp.float32)
+                hop(1, me, chunk, me).wait_recv()
+                out_ref[place, :] += held[1, me, chunk].astype(jnp.float32)
 
         for step in range(count - 1):
             for way, owner, inside in flows(step):
 
                 @pl.when(inside)
                 def _():
-                    hop(way, owner, me).wait_send()
+                    for chunk in range(CHUNKS):
+                        hop(way, owner, chunk, me).wait_send()
 
     return [functools.partial(move, step) for step in range(count - 1)] + [last]
 
@@ -422,7 +431,7 @@
     )
 
 
-def chain_kernel(kind, split, shared, count, dp_count, sizes, *refs):
+def chain_kernel(kind, splits, shared, count, dp_count, sizes, *refs):
     me = lax.axis_index("col")
     refs = list(refs)
 
@@ -431,47 +440,48 @@
         del refs[:number]
         return taken
 
-    extras = (split is not None) + (shared > 0)
+    extras = len(splits) + (shared > 0)
     inputs, outputs = pull(1 + extras), pull(1 + extras)
     greet(me, count, reduce_levels(dp_count) if extras else [], shared > 0)
-    chain = (gather_stages if kind == "gather" else scatter_stages)(
-        count, inputs[0], outputs[0], *pull(sizes[0])
-    )
-    weight, vector = [], []
-    if split is not None:
-        weight = weight_stages(split, dp_count, inputs[1], outputs[1], pull(sizes[1]))
+    lines = [
+        (gather_stages if kind == "gather" else scatter_stages)(
+            count, inputs[0], outputs[0], *pull(sizes[0])
+        )
+    ]
+    for place, split in enumerate(splits):
+        lines.append(
+            weight_stages(
+                split, dp_count, inputs[1 + place], outputs[1 + place], pull(sizes[1 + place])
+            )
+        )
     if shared > 0:
-        vector = vector_stages(count, dp_count, shared, inputs[2], outputs[2], *pull(sizes[2]))
-    order = []
-    for position in range(max(len(chain), len(weight), len(vector))):
-        if position < len(chain):
-            order.append(chain[position])
-        if position < len(vector):
-            order.append(vector[position])
-        if position < len(weight):
-            order.append(weight[position])
-    for stage in order:
-        stage()
-
-
-def chain_call(kind, ident, block, weight=None, split=None, vectors=None, shared=0):
+        lines.append(
+            vector_stages(count, dp_count, shared, inputs[-1], outputs[-1], *pull(sizes[-1]))
+        )
+    for position in range(max(len(line) for line in lines)):
+        for line in lines:
+            if position < len(line):
+                line[position]()
+
+
+def chain_call(kind, ident, block, weights=(), splits=(), vectors=None, shared=0):
     count, dp_count = lax.axis_size("col"), lax.axis_size("dp")
     rows, width = block.shape
-    operands, sizes = [block], [0, 0, 0]
+    operands, sizes = [block], []
     if kind == "gather":
         shapes = [jax.ShapeDtypeStruct((count * rows, width), block.dtype)]
         scratch = [pltpu.SemaphoreType.DMA((2, count - 1))] * 2
     else:
         rows //= count
         shapes = [jax.ShapeDtypeStruct((rows, width), jnp.float32)]
-        scratch = [pltpu.VMEM((2, count, rows, width), jnp.bfloat16)] * 2
-        scratch += [pltpu.SemaphoreType.DMA((2, count))] * 2
-    sizes[0] = len(scratch)
-    if weight is not None:
+        scratch = [pltpu.VMEM((2, count, CHUNKS, rows // CHUNKS, width), jnp.bfloat16)] * 2
+        scratch += [pltpu.SemaphoreType.DMA((2, count, CHUNKS))] * 2
+    sizes.append(len(scratch))
+    for weight, split in zip(weights, splits):
         operands.append(weight)
         shapes.append(jax.ShapeDtypeStruct(weight_shape(weight.shape, split), jnp.float32))
         more = weight_scratch(weight.shape, split, dp_count)
-        sizes[1] = len(more)
+        sizes.append(len(more))
         scratch += more
     if vectors is not None:
         operands.append(vectors)
@@ -484,10 +494,10 @@
             pltpu.SemaphoreType.DMA((levels + count,)),
             pltpu.SemaphoreType.DMA((levels + count,)),
         ]
-        sizes[2] = len(more)
+        sizes.append(len(more))
         scratch += more
     results = pl.pallas_call(
-        functools.partial(chain_kernel, kind, split, shared, count, dp_count, tuple(sizes)),
+        functools.partial(chain_kernel, kind, tuple(splits), shared, count, dp_count, tuple(sizes)),
         out_shape=shapes,
         in_specs=[pl.BlockSpec(memory_space=pltpu.VMEM)] * len(operands),
         out_specs=[pl.BlockSpec(memory_space=pltpu.VMEM)] * len(operands),
@@ -608,11 +618,12 @@
     return jnp.stack([grad_query, grad_keys, grad_values], axis=2)
 
 
-def weight_total(part, dimension):
-    part = lax.psum_scatter(
-        part.astype(jnp.bfloat16), "row", scatter_dimension=dimension, tiled=True
-    )
-    return lax.psum(part, "dp").astype(jnp.float32)
+def both_halves(half, dimension):
+    other = lax.ppermute(half, "row", [(0, 1), (1, 0)])
+    ahead = lax.axis_index("row") == 0
+    return jnp.concatenate(
+        [jnp.where(ahead, half, other), jnp.where(ahead, other, half)], axis=dimension
+    )
 
 
 def per_device(
@@ -641,10 +652,10 @@
     vectors = jnp.stack(
         [mixer_bias, first_gain, first_shift, narrow_bias, second_gain, second_shift]
     )
-    vectors = lax.all_gather(vectors, "row", axis=1, tiled=True)
+    vectors = both_halves(vectors, 1)
     mixer_bias, first_gain, first_shift, narrow_bias, second_gain, second_shift = vectors
-    attend_weight = lax.all_gather(attend_weight, "row", axis=0, tiled=True)
-    mixer_weight = lax.all_gather(mixer_weight, "row", axis=1, tiled=True)
+    attend_weight = both_halves(attend_weight, 0)
+    mixer_weight = both_halves(mixer_weight, 1)
     widen_weight = lax.all_gather(widen_weight, "row", axis=0, tiled=True)
     narrow_weight = lax.all_gather(narrow_weight, "row", axis=1, tiled=True)
 
@@ -688,18 +699,22 @@
     grad_active = outer_back(grad_narrow_block, narrow_weight)
     grad_widened = gelu_pull(grad_active)[0].astype(jnp.bfloat16)
     widen_bias_part = jnp.sum(grad_widened, axis=0, dtype=jnp.float32)
-    grad_first, narrow_total = chain_call(
-        "scatter", 2, outer_back(grad_widened, widen_weight), narrow_part, 1
+    widen_part = inner_rows(gathered_first, grad_widened).astype(jnp.bfloat16)
+    grad_first, narrow_total, widen_total = chain_call(
+        "scatter",
+        2,
+        outer_back(grad_widened, widen_weight),
+        (narrow_part, widen_part),
+        (1, 0),
     )
     grad_first = grad_first + grad_second
-    widen_part = inner_rows(gathered_first, grad_widened).astype(jnp.bfloat16)
     first_gain_part = jnp.sum(grad_first * first_normal, axis=0)
     first_shift_part = jnp.sum(grad_first, axis=0)
     grad_attended = norm_backward(grad_first, first_normal, first_inverse, first_gain)
     grad_mix = grad_attended.astype(jnp.bfloat16)
     mixer_bias_part = jnp.sum(grad_mix, axis=0, dtype=jnp.float32)
-    grad_mixer_block, widen_total = chain_call("gather", 3, grad_mix, widen_part, 0)
-    mixer_total = weight_total(inner_rows(mixed_block, grad_mixer_block), 1)
+    grad_mixer_block = gather_tokens(grad_mix)
+    mixer_part = inner_rows(grad_mixer_block, mixed_block).astype(jnp.bfloat16)
     grad_mixed = outer_back(grad_mixer_block, mixer_weight).astype(jnp.bfloat16)
     grad_heads = grad_mixed.reshape(slot_rows, heads_here, HD)
     grad_slots = slot_backward((query_all, keys_all, values_all, length, logsum, grad_heads))
@@ -721,10 +736,18 @@
             jnp.pad(attend_bias_flat, (0, model - attend_bias_flat.shape[0])),
         ]
     )
-    input_gradient, attend_total, vector_sums = chain_call(
-        "scatter", 4, outer_back(grad_packed, attend_weight), attend_part, 0, vector_parts, 6
-    )
-    input_gradient = from_slot_rows(input_gradient + grad_attended)
+    input_gradient, attend_total, mixer_total, vector_sums = chain_call(
+        "scatter",
+        3,
+        outer_back(grad_packed, attend_weight),
+        (attend_part, mixer_part),
+        (0, 0),
+        vector_parts,
+        6,
+    )
+    mixer_total = mixer_total.T
+    input_gradient = from_slot_rows((input_gradient + grad_attended).astype(jnp.bfloat16))
+    input_gradient = input_gradient.astype(jnp.float32)
     half = model // 2
     vector_totals = lax.dynamic_slice_in_dim(vector_sums, row_rank * half, half, 1)
     column_totals = (

time: 408 us -> 389 us (0.953)
  blocking collectives: 19.2 us -> 0 us
  Pallas kernels: 249 us -> 257 us
  matrix products: 40.3 us -> 33.4 us
  other arithmetic: 13.8 us -> 8.22 us
  starting transfers between devices: 17.5 us -> 21.6 us
    ppermute x0 -> x3, waiting for transfers between devices: none -> 24.7 us  [both_halves(): other = lax.ppermute(half, 'row', [(0, 1), (1, 0)])]
    all_gather x2 -> x0, blocking collectives: 19.2 us -> none  [the longest x1 14.4 us: per_device(): mixer_weight = lax.all_gather(mixer_weight, 'row', axis=1, tiled=True)]
    ppermute x4, waiting for transfers between devices: 22.1 us -> 9.39 us  [from_slot_rows(): landed.append(lax.ppermute(piece, ('row', 'col'), pairs))]
    psum x1 -> x0, waiting for transfers between devices: 11.6 us -> none  [weight_total(): return lax.psum(part, 'dp').astype(jnp.float32)]
    pallas_call x8, Pallas kernels: 249 us -> 257 us  [chain_call(): pl.pallas_call(functools.partial(chain_kernel, kind, tuple(splits), share...]
    unnamed x81 -> x64, local copies, waits for them, and re-layouts: 11.1 us -> 13.1 us
  transfers between devices with their start and end apart: 13 -> 13, of which waited for: 3 -> 3; matrix products, arithmetic and copies ran while one was open for 7% -> 6% of each run, Pallas kernels for 27% -> 30%
where the time goes in v3:
time: 389 us
  Pallas kernels  257 us (66%)
  waiting for transfers between devices  34.8 us (9%)
  matrix products  33.4 us (9%)
  starting transfers between devices  21.6 us (6%)
  local copies, waits for them, and re-layouts  19.2 us (5%)
  between operations  14.8 us (4%)
  other arithmetic  8.22 us (2%)
    pallas_call x8, Pallas kernels, chain_call(): pl.pallas_call(functools.partial(chain_kernel, kind, tuple(splits), share...  257 us
    ppermute x3, waiting for transfers between devices, both_halves(): other = lax.ppermute(half, 'row', [(0, 1), (1, 0)])  24.7 us
    dot_general x4, matrix products, product(): return jnp.dot(left_side, right_side, preferred_element_type=jnp.float32)  13.3 us
    unnamed x64, local copies, waits for them, and re-layouts  13.1 us
    ppermute x4, starting transfers between devices, to_slot_rows(): landed.append(lax.ppermute(block, ('row', 'col'), slot_moves(swap)))  9.92 us
    ppermute x4, waiting for transfers between devices, from_slot_rows(): landed.append(lax.ppermute(piece, ('row', 'col'), pairs))  9.39 us
    dot_general x4, matrix products, inner_rows(): lax.dot_general(left_side, right_side, (((0,), (0,)), ((), ())), preferre...  7.97 us
    ppermute x4, starting transfers between devices, from_slot_rows(): landed.append(lax.ppermute(piece, ('row', 'col'), pairs))  7.92 us
  transfers between devices with their start and end apart: 13, of which 3 were waited for; matrix products, arithmetic and copies ran while one was open for 6% of the time, Pallas kernels for 30%

profile of v3, /device:TPU:8, one launch (start us, length us, event | category | flops | bytes accessed | tf_op | source)
XLA Modules:
  0.0 389.0 jit_solution(15394834072593891101)
XLA Ops:
  8.8 1.6 collective-permute-start.4
  11.4 2.6 collective-permute-start
  14.0 1.9 collective-permute-start.1
  17.5 4.8 %collective-permute-start.8 = (bf16[128,512]{1,0:T(8,128)(2,1)S(1)}, bf16[128,512]{1,0:T(8,128)(2,1)S(1)}, u32[]{:S(2)}, u32[]{:S(2)}) collective-permute-start(bf16[128,512]{1,0:T(8,128)(2,1)S(1)} %get-tuple-element.107), channel_id=1, source_target_pairs={{0,0},{1,2},{2,4},{3,6},{4,1},{5,3},{6,5},{7,7},{8,8},{9,10},{10,1... | collective-permute-start | bytes 393224 | tf_op jit(solution)/shard_map/ppermute | solution.py:541
  24.7 2.1 collective-permute-start.3
  26.8 17.9 %chain_gather0.4 = bf16[512,1024]{1,0:T(8,128)(2,1)S(1)} custom-call(bf16[128,1024]{1,0:T(8,128)(2,1)S(1)} %pad_maximum_fusion.6.refs_0_), custom_call_target="tpu_custom_call" | custom-call | bytes 62914560 | tf_op jit(solution)/shard_map/chain_gather0/pallas_call | solution.py:499
  44.8 24.7 %collective-permute-done.3 = bf16[256,512]{1,0:T(8,128)(2,1)S(1)} collective-permute-done((bf16[256,512]{1,0:T(8,128)(2,1)S(1)}, bf16[256,512]{1,0:T(8,128)(2,1)S(1)}, u32[]{:S(2)}, u32[]{:S(2)}) %collective-permute-start.3) | collective-permute-done | bytes 262176 | tf_op jit(solution)/shard_map/ppermute | solution.py:622
  73.7 1.4 copy-done.7
  76.4 28.9 %chain_scatter1.2 = f32[128,1024]{1,0:T(8,128)S(1)} custom-call(f32[512,1024]{1,0:T(8,128)S(1)} %fusion.23.refs_0_), custom_call_target="tpu_custom_call" | custom-call | bytes 62914560 | tf_op jit(solution)/shard_map/chain_scatter1/pallas_call | solution.py:499
  106.0 17.3 %chain_gather0.5 = bf16[512,1024]{1,0:T(8,128)(2,1)S(1)} custom-call(bf16[128,1024]{1,0:T(8,128)(2,1)S(1)} %fusion.22.refs_0_), custom_call_target="tpu_custom_call" | custom-call | bytes 62914560 | tf_op jit(solution)/shard_map/chain_gather0/pallas_call | solution.py:499
  123.3 8.7 %multiply_convert_fusion.1 = (bf16[512,1024]{1,0:T(8,128)(2,1)}, f32[512,1024]{1,0:T(8,128)}, f32[512,1024]{1,0:T(8,128)}) fusion(f32[1024]{0:T(1024)S(1)} %copy-done.25, bf16[512,1024]{1,0:T(8,128)(2,1)S(1)} %chain_gather0.5, bf16[1024,1024]{1,0:T(8,128)(2,1)} %all-gather.3.cloned.1.call-done), kind=kOutput, calls=%fused_computation.14 | convolution fusion | flops 1108344832 | bytes 8392704 | tf_op jit(solution)/shard_map/dot_general | solution.py:19
  132.1 3.2 fusion.35.refs_0_
  135.3 30.6 %chain_scatter1.3 = f32[128,1024]{1,0:T(8,128)S(1)} custom-call(f32[512,1024]{1,0:T(8,128)S(1)} %fusion.35.refs_0_), custom_call_target="tpu_custom_call" | custom-call | bytes 62914560 | tf_op jit(solution)/shard_map/chain_scatter1/pallas_call | solution.py:499
  167.1 17.5 %chain_gather0.6 = bf16[512,1024]{1,0:T(8,128)(2,1)S(1)} custom-call(bf16[128,1024]{1,0:T(8,128)(2,1)S(1)} %get-tuple-element.83.refs_0_), custom_call_target="tpu_custom_call" | custom-call | bytes 62914560 | tf_op jit(solution)/shard_map/chain_gather0/pallas_call | solution.py:499
  184.6 2.7 convolution_convert_fusion.1.refs_1_
  188.2 1.9 convert_reduce_fusion
  190.2 2.6 convolution_convert_fusion.refs_2_
  192.8 2.6 fusion.36.refs_0_
  195.4 73.0 %chain_scatter2.1 = (f32[128,1024]{1,0:T(8,128)S(1)}, f32[1024,512]{1,0:T(8,128)S(1)}, f32[512,1024]{1,0:T(8,128)S(1)}) custom-call(f32[512,1024]{1,0:T(8,128)} %fusion.36.refs_0_, bf16[1024,1024]{1,0:T(8,128)(2,1)} %convolution_convert_fusion.1.refs_1_, bf16[1024,1024]{1,0:T(8,128)(2,1)} %convolution_convert_fusion.refs_2_), custom_call_target="tpu_custom_call" | custom-call | bytes 62914560 | tf_op jit(solution)/shard_map/chain_scatter2/pallas_call | solution.py:499
  269.9 20.6 %chain_gather0.7 = bf16[512,1024]{1,0:T(8,128)(2,1)S(1)} custom-call(bf16[128,1024]{1,0:T(8,128)(2,1)S(1)} %get-tuple-element.86.refs_0_), custom_call_target="tpu_custom_call" | custom-call | bytes 62914560 | tf_op jit(solution)/shard_map/chain_gather0/pallas_call | solution.py:499
  291.5 1.2 copy-done.8
  298.0 2.2 convolution_convert_fusion.2.refs_1_
  300.2 2.4 fusion.18.refs_0_
  303.3 2.5 collective-permute-start.5
  305.8 2.5 collective-permute-start.6
  308.4 1.4 copy-done.4
  309.8 51.0 %chain_scatter3.1 = (f32[128,1024]{1,0:T(8,128)S(1)}, f32[512,768]{1,0:T(8,128)S(1)}, f32[512,256]{1,0:T(8,128)S(1)}, f32[8,1024]{1,0:T(8,128)S(1)}) custom-call(f32[512,1024]{1,0:T(8,128)} %fusion.18.refs_0_, bf16[1024,768]{1,0:T(8,128)(2,1)S(1)} %copy-done.4, bf16[1024,256]{1,0:T(8,128)(2,1)S(1)} %convolution_convert_fusion.3.refs_2_, ...), custom_call_target="tpu_custom_call" | custom-call | bytes 62914560 | tf_op jit(solution)/shard_map/chain_scatter3/pallas_call | solution.py:499
  362.6 3.0 collective-permute-start.10
  369.1 8.4 %collective-permute-done.10 = bf16[128,512]{1,0:T(8,128)(2,1)S(1)} collective-permute-done((bf16[128,512]{1,0:T(8,128)(2,1)S(1)}, bf16[128,512]{1,0:T(8,128)(2,1)S(1)}, u32[]{:S(2)}, u32[]{:S(2)}) %collective-permute-start.10) | collective-permute-done | bytes 131104 | tf_op jit(solution)/shard_map/ppermute | solution.py:555
  378.3 1.1 copy.69
  379.5 1.3 copy.70
  380.8 1.3 copy.71
  (139 shorter events, 29.2 us)
Async XLA Ops:
  7.2 15.2 %copy-start.26 = (s32[2]{0:T(128)S(1)}, s32[2]{0:T(128)}, u32[]{:S(2)}) copy-start(s32[2]{0:T(128)} %param.16) | copy-start | bytes 28
  7.2 16.4 %copy-start.22 = (f32[4,128]{1,0:T(4,128)S(1)}, f32[4,128]{1,0:T(4,128)}, u32[]{:S(2)}) copy-start(f32[4,128]{1,0:T(4,128)} %param.18) | copy-start | bytes 6148
  7.2 17.4 %copy-start.16 = (bf16[512,768]{1,0:T(8,128)(2,1)S(1)}, bf16[512,768]{1,0:T(8,128)(2,1)}, u32[]{:S(2)}) copy-start(bf16[512,768]{1,0:T(8,128)(2,1)} %param.17) | copy-start | bytes 2359300
  7.2 17.4 %copy-start.21 = (bf16[256,512]{1,0:T(8,128)(2,1)S(1)}, bf16[256,512]{1,0:T(8,128)(2,1)}, u32[]{:S(2)}) copy-start(bf16[256,512]{1,0:T(8,128)(2,1)} %param.19) | copy-start | bytes 786436
  7.2 116.1 %all-gather.3.cloned.1.call-start = ((), (), s32[]{:S(2)}) async-start(), calls=%async_computation | async-start | bytes 3145728 | tf_op jit(solution)/shard_map/all_gather | solution.py:659
  8.0 124.1 %all-gather.5.cloned.1.call-start = ((), (), s32[]{:S(2)}) async-start(), calls=%async_computation.1 | async-start | bytes 3145728 | tf_op jit(solution)/shard_map/all_gather | solution.py:660
  8.8 15.8 %collective-permute-start.4 = (f32[6,512]{1,0:T(8,128)S(1)}, f32[6,512]{1,0:T(8,128)S(1)}, u32[]{:S(2)}, u32[]{:S(2)}) collective-permute-start(f32[6,512]{1,0:T(8,128)S(1)} %stack.66), channel_id=1, source_target_pairs={{0,4},{4,0},{1,5},{5,1},{2,6},{6,2},{3,7},{7,3},{8,12},{12,8},{9,1... | collective-permute-start | bytes 36872 | tf_op jit(solution)/shard_map/ppermute | solution.py:622
  11.4 13.3 %collective-permute-start = (bf16[128,512]{1,0:T(8,128)(2,1)S(1)}, bf16[128,512]{1,0:T(8,128)(2,1)S(1)}, u32[]{:S(2)}, u32[]{:S(2)}) collective-permute-start(bf16[128,512]{1,0:T(8,128)(2,1)S(1)} %get-tuple-element.114), channel_id=1, source_target_pairs={{0,1},{1,3},{2,5},{3,7},{4,0},{5,2},{6,4},{7,6},{8,9},{9,11},{10,1... | collective-permute-start | bytes 393224 | tf_op jit(solution)/shard_map/ppermute | solution.py:541
  14.0 12.7 %collective-permute-start.1 = (bf16[128,512]{1,0:T(8,128)(2,1)S(1)}, bf16[128,512]{1,0:T(8,128)(2,1)S(1)}, u32[]{:S(2)}, u32[]{:S(2)}) collective-permute-start(bf16[128,512]{1,0:T(8,128)(2,1)S(1)} %get-tuple-element.115), channel_id=1, source_target_pairs={{0,0},{1,2},{2,4},{3,6},{4,1},{5,3},{6,5},{7,7},{8,8},{9,10},{10,1... | collective-permute-start | bytes 393224 | tf_op jit(solution)/shard_map/ppermute | solution.py:541
  16.9 9.8 %collective-permute-start.7 = (bf16[128,512]{1,0:T(8,128)(2,1)S(1)}, bf16[128,512]{1,0:T(8,128)(2,1)S(1)}, u32[]{:S(2)}, u32[]{:S(2)}) collective-permute-start(bf16[128,512]{1,0:T(8,128)(2,1)S(1)} %get-tuple-element.106), channel_id=1, source_target_pairs={{0,1},{1,3},{2,5},{3,7},{4,0},{5,2},{6,4},{7,6},{8,9},{9,11},{10,1... | collective-permute-start | bytes 393224 | tf_op jit(solution)/shard_map/ppermute | solution.py:541
  17.5 9.3 %collective-permute-start.8 = (bf16[128,512]{1,0:T(8,128)(2,1)S(1)}, bf16[128,512]{1,0:T(8,128)(2,1)S(1)}, u32[]{:S(2)}, u32[]{:S(2)}) collective-permute-start(bf16[128,512]{1,0:T(8,128)(2,1)S(1)} %get-tuple-element.107), channel_id=1, source_target_pairs={{0,0},{1,2},{2,4},{3,6},{4,1},{5,3},{6,5},{7,7},{8,8},{9,10},{10,1... | collective-permute-start | bytes 393224 | tf_op jit(solution)/shard_map/ppermute | solution.py:541
  24.6 45.0 %collective-permute-start.2 = (bf16[512,768]{1,0:T(8,128)(2,1)S(1)}, bf16[512,768]{1,0:T(8,128)(2,1)S(1)}, u32[]{:S(2)}, u32[]{:S(2)}) collective-permute-start(bf16[512,768]{1,0:T(8,128)(2,1)S(1)} %copy-done.16), channel_id=1, source_target_pairs={{0,4},{4,0},{1,5},{5,1},{2,6},{6,2},{3,7},{7,3},{8,12},{12,8},{9,1... | collective-permute-start | bytes 2359304 | tf_op jit(solution)/shard_map/ppermute | solution.py:622
  24.7 44.8 %collective-permute-start.3 = (bf16[256,512]{1,0:T(8,128)(2,1)S(1)}, bf16[256,512]{1,0:T(8,128)(2,1)S(1)}, u32[]{:S(2)}, u32[]{:S(2)}) collective-permute-start(bf16[256,512]{1,0:T(8,128)(2,1)S(1)} %copy-done.21), channel_id=1, source_target_pairs={{0,4},{4,0},{1,5},{5,1},{2,6},{6,2},{3,7},{7,3},{8,12},{12,8},{9,1... | collective-permute-start | bytes 786440 | tf_op jit(solution)/shard_map/ppermute | solution.py:622
  44.8 24.9 %copy-start.5 = (bf16[512,1024]{1,0:T(8,128)(2,1)}, bf16[512,1024]{1,0:T(8,128)(2,1)S(1)}, u32[]{:S(2)}) copy-start(bf16[512,1024]{1,0:T(8,128)(2,1)S(1)} %chain_gather0.4) | copy-start | bytes 3145732
  69.5 6.4 %copy-start.12 = (bf16[256,512]{1,0:T(8,128)(2,1)}, bf16[256,512]{1,0:T(8,128)(2,1)S(1)}, u32[]{:S(2)}) copy-start(bf16[256,512]{1,0:T(8,128)(2,1)S(1)} %get-tuple-element.98) | copy-start | bytes 786436
  69.6 6.4 %copy-start.14 = (bf16[256,512]{1,0:T(8,128)(2,1)}, bf16[256,512]{1,0:T(8,128)(2,1)S(1)}, u32[]{:S(2)}) copy-start(bf16[256,512]{1,0:T(8,128)(2,1)S(1)} %get-tuple-element.99) | copy-start | bytes 786436
  76.0 29.4 %copy-start.10 = (bf16[4,64,512]{2,1,0:T(8,128)(2,1)}, bf16[4,64,512]{2,1,0:T(8,128)(2,1)S(1)}, u32[]{:S(2)}) copy-start(bf16[4,64,512]{2,1,0:T(8,128)(2,1)S(1)} %fusion.17) | copy-start | bytes 786436
  105.4 17.9 %copy-start.25 = (f32[1024]{0:T(1024)S(1)}, f32[1024]{0:T(1024)}, u32[]{:S(2)}) copy-start(f32[1024]{0:T(1024)} %param.24) | copy-start | bytes 12292
  166.4 18.2 %copy-start.27 = (bf16[512,1024]{1,0:T(8,128)(2,1)S(1)}, bf16[512,1024]{1,0:T(8,128)(2,1)}, u32[]{:S(2)}) copy-start(bf16[512,1024]{1,0:T(8,128)(2,1)} %get-tuple-element.91) | copy-start | bytes 3145732
  184.6 2.7 copy-start.24
  184.6 2.7 copy-start.28
  184.6 3.6 copy-start.29
  190.2 2.6 copy-start.23
  268.8 21.8 %copy-start.13 = (bf16[256,512]{1,0:T(8,128)(2,1)S(1)}, bf16[256,512]{1,0:T(8,128)(2,1)}, u32[]{:S(2)}) copy-start(bf16[256,512]{1,0:T(8,128)(2,1)} %copy-done.12) | copy-start | bytes 786436
  268.8 21.8 %copy-start.15 = (bf16[256,512]{1,0:T(8,128)(2,1)S(1)}, bf16[256,512]{1,0:T(8,128)(2,1)}, u32[]{:S(2)}) copy-start(bf16[256,512]{1,0:T(8,128)(2,1)} %copy-done.14) | copy-start | bytes 786436
  269.9 21.1 %copy-start.11 = (bf16[4,64,512]{2,1,0:T(8,128)(2,1)S(1)}, bf16[4,64,512]{2,1,0:T(8,128)(2,1)}, u32[]{:S(2)}) copy-start(bf16[4,64,512]{2,1,0:T(8,128)(2,1)} %copy-done.10) | copy-start | bytes 786436
  303.3 64.0 %collective-permute-start.5 = (bf16[128,512]{1,0:T(8,128)(2,1)}, bf16[128,512]{1,0:T(8,128)(2,1)S(1)}, u32[]{:S(2)}, u32[]{:S(2)}) collective-permute-start(bf16[128,512]{1,0:T(8,128)(2,1)} %get-tuple-element.110), channel_id=1, source_target_pairs={{1,0},{3,1},{5,2},{7,3},{0,4},{2,5},{4,6},{6,7},{9,8},{11,9},{13,1... | collective-permute-start | bytes 393224 | tf_op jit(solution)/shard_map/ppermute | solution.py:555
  305.8 61.5 %collective-permute-start.6 = (bf16[128,512]{1,0:T(8,128)(2,1)}, bf16[128,512]{1,0:T(8,128)(2,1)S(1)}, u32[]{:S(2)}, u32[]{:S(2)}) collective-permute-start(bf16[128,512]{1,0:T(8,128)(2,1)} %get-tuple-element.111), channel_id=1, source_target_pairs={{0,0},{2,1},{4,2},{6,3},{1,4},{3,5},{5,6},{7,7},{8,8},{10,9},{12,1... | collective-permute-start | bytes 393224 | tf_op jit(solution)/shard_map/ppermute | solution.py:555
  309.8 52.1 %copy-start.9 = (f32[128,1024]{1,0:T(8,128)S(1)}, f32[128,1024]{1,0:T(8,128)}, u32[]{:S(2)}) copy-start(f32[128,1024]{1,0:T(8,128)} %get-tuple-element.87) | copy-start | bytes 1572868
  362.6 6.5 %collective-permute-start.9 = (bf16[128,512]{1,0:T(8,128)(2,1)S(1)}, bf16[128,512]{1,0:T(8,128)(2,1)S(1)}, u32[]{:S(2)}, u32[]{:S(2)}) collective-permute-start(bf16[128,512]{1,0:T(8,128)(2,1)S(1)} %get-tuple-element.102), channel_id=1, source_target_pairs={{1,0},{3,1},{5,2},{7,3},{0,4},{2,5},{4,6},{6,7},{9,8},{11,9},{13,1... | collective-permute-start | bytes 393224 | tf_op jit(solution)/shard_map/ppermute | solution.py:555
  362.6 14.8 %collective-permute-start.10 = (bf16[128,512]{1,0:T(8,128)(2,1)S(1)}, bf16[128,512]{1,0:T(8,128)(2,1)S(1)}, u32[]{:S(2)}, u32[]{:S(2)}) collective-permute-start(bf16[128,512]{1,0:T(8,128)(2,1)S(1)} %get-tuple-element.103), channel_id=1, source_target_pairs={{0,0},{2,1},{4,2},{6,3},{1,4},{3,5},{5,6},{7,7},{8,8},{10,9},{12,1... | collective-permute-start | bytes 393224 | tf_op jit(solution)/shard_map/ppermute | solution.py:555
  366.6 11.7 %copy-start.3 = (f32[512,768]{1,0:T(8,128)S(1)}, f32[512,768]{1,0:T(8,128)}, u32[]{:S(2)}) copy-start(f32[512,768]{1,0:T(8,128)} %copy-done.2) | copy-start | bytes 4718596
  (11 other events, 18.0 us)
Sparse Core Ops, SparseCore 0:
  9.6 58.2 all-gather.2
  69.5 32.7 all-gather.4

commit v4 on v3

--- a/solution.py
+++ b/solution.py
@@ -656,6 +656,9 @@
     mixer_bias, first_gain, first_shift, narrow_bias, second_gain, second_shift = vectors
     attend_weight = both_halves(attend_weight, 0)
     mixer_weight = both_halves(mixer_weight, 1)
+    input_block, widen_weight, narrow_weight = lax.optimization_barrier(
+        (input_block, widen_weight, narrow_weight)
+    )
     widen_weight = lax.all_gather(widen_weight, "row", axis=0, tiled=True)
     narrow_weight = lax.all_gather(narrow_weight, "row", axis=1, tiled=True)
 

time: 389 us -> 390 us (level)
  waiting for transfers between devices: 34.8 us -> 30.2 us
    ppermute x3, waiting for transfers between devices: 24.7 us -> 16.8 us  [both_halves(): other = lax.ppermute(half, 'row', [(0, 1), (1, 0)])]
    unnamed x64 -> x76, local copies, waits for them, and re-layouts: 13.1 us -> 13 us
  transfers between devices with their start and end apart: 13 -> 13, of which waited for: 3 -> 4; matrix products, arithmetic and copies ran while one was open for 6% -> 6% of each run, Pallas kernels for 30% -> 30%
where the time goes in v4:
time: 390 us; the launch traced here: 389 us
  Pallas kernels  257 us (66%)
  matrix products  34.9 us (9%)
  waiting for transfers between devices  30.2 us (8%)
  starting transfers between devices  21.4 us (5%)
  local copies, waits for them, and re-layouts  20.2 us (5%)
  between operations  14.8 us (4%)
  other arithmetic  10.6 us (3%)
    pallas_call x8, Pallas kernels, chain_call(): pl.pallas_call(functools.partial(chain_kernel, kind, tuple(splits), share...  257 us
    ppermute x3, waiting for transfers between devices, both_halves(): other = lax.ppermute(half, 'row', [(0, 1), (1, 0)])  16.8 us
    dot_general x4, matrix products, product(): return jnp.dot(left_side, right_side, preferred_element_type=jnp.float32)  14.2 us
    unnamed x76, local copies, waits for them, and re-layouts  13 us
    ppermute x4, starting transfers between devices, to_slot_rows(): landed.append(lax.ppermute(block, ('row', 'col'), slot_moves(swap)))  10.9 us
    ppermute x4, waiting for transfers between devices, from_slot_rows(): landed.append(lax.ppermute(piece, ('row', 'col'), pairs))  10.2 us
    dot_general x4, matrix products, outer_back(): lax.dot_general(left_side, right_side, (((1,), (1,)), ((), ())), preferre...  7.97 us
    dot_general x4, matrix products, inner_rows(): lax.dot_general(left_side, right_side, (((0,), (0,)), ((), ())), preferre...  7.96 us
  transfers between devices with their start and end apart: 13, of which 4 were waited for; matrix products, arithmetic and copies ran while one was open for 6% of the time, Pallas kernels for 30%

profile of v4, /device:TPU:8, one launch (start us, length us, event | category | flops | bytes accessed | tf_op | source)
XLA Modules:
  0.0 389.1 jit_solution(474542839683396207)
XLA Ops:
  8.4 2.6 collective-permute-start
  11.1 2.3 collective-permute-start.1
  14.4 1.4 collective-permute-start.7
  15.8 4.6 %collective-permute-start.8 = (bf16[128,512]{1,0:T(8,128)(2,1)S(1)}, bf16[128,512]{1,0:T(8,128)(2,1)S(1)}, u32[]{:S(2)}, u32[]{:S(2)}) collective-permute-start(bf16[128,512]{1,0:T(8,128)(2,1)S(1)} %get-tuple-element.113), channel_id=1, source_target_pairs={{0,0},{1,2},{2,4},{3,6},{4,1},{5,3},{6,5},{7,7},{8,8},{9,10},{10,1... | collective-permute-start | bytes 393224 | tf_op jit(solution)/shard_map/ppermute | solution.py:541
  20.4 3.1 collective-permute-done.8
  29.3 18.7 %chain_gather0.4 = bf16[512,1024]{1,0:T(8,128)(2,1)S(1)} custom-call(bf16[128,1024]{1,0:T(8,128)(2,1)S(1)} %pad_maximum_fusion.6.refs_0_), custom_call_target="tpu_custom_call" | custom-call | bytes 62914560 | tf_op jit(solution)/shard_map/chain_gather0/pallas_call | solution.py:499
  48.1 16.8 %collective-permute-done.2 = bf16[512,768]{1,0:T(8,128)(2,1)} collective-permute-done((bf16[512,768]{1,0:T(8,128)(2,1)S(1)}, bf16[512,768]{1,0:T(8,128)(2,1)}, u32[]{:S(2)}, u32[]{:S(2)}) %collective-permute-start.2) | collective-permute-done | bytes 786464 | tf_op jit(solution)/shard_map/ppermute | solution.py:622
  67.4 1.9 add_convert_fusion.1
  69.3 1.4 copy.49
  72.3 1.3 copy-done.7
  74.9 30.5 %chain_scatter1.2 = f32[128,1024]{1,0:T(8,128)S(1)} custom-call(f32[512,1024]{1,0:T(8,128)S(1)} %fusion.23.refs_0_), custom_call_target="tpu_custom_call" | custom-call | bytes 62914560 | tf_op jit(solution)/shard_map/chain_scatter1/pallas_call | solution.py:499
  106.0 17.3 %chain_gather0.5 = bf16[512,1024]{1,0:T(8,128)(2,1)S(1)} custom-call(bf16[128,1024]{1,0:T(8,128)(2,1)S(1)} %fusion.22.refs_0_), custom_call_target="tpu_custom_call" | custom-call | bytes 62914560 | tf_op jit(solution)/shard_map/chain_gather0/pallas_call | solution.py:499
  123.4 8.7 %multiply_convert_fusion.1 = (bf16[512,1024]{1,0:T(8,128)(2,1)}, f32[512,1024]{1,0:T(8,128)}, f32[512,1024]{1,0:T(8,128)}) fusion(f32[1024]{0:T(1024)S(1)} %copy-done.31, bf16[512,1024]{1,0:T(8,128)(2,1)S(1)} %chain_gather0.5, bf16[1024,1024]{1,0:T(8,128)(2,1)} %all-gather.3.cloned.1.call-done), kind=kOutput, calls=%fused_computation.14 | convolution fusion | flops 1108344832 | bytes 8392704 | tf_op jit(solution)/shard_map/dot_general | solution.py:19
  132.1 3.2 fusion.35.refs_0_
  135.3 28.3 %chain_scatter1.3 = f32[128,1024]{1,0:T(8,128)S(1)} custom-call(f32[512,1024]{1,0:T(8,128)S(1)} %fusion.35.refs_0_), custom_call_target="tpu_custom_call" | custom-call | bytes 62914560 | tf_op jit(solution)/shard_map/chain_scatter1/pallas_call | solution.py:499
  164.8 17.5 %chain_gather0.6 = bf16[512,1024]{1,0:T(8,128)(2,1)S(1)} custom-call(bf16[128,1024]{1,0:T(8,128)(2,1)S(1)} %get-tuple-element.89.refs_0_), custom_call_target="tpu_custom_call" | custom-call | bytes 62914560 | tf_op jit(solution)/shard_map/chain_gather0/pallas_call | solution.py:499
  182.4 2.7 convolution_convert_fusion.1.refs_1_
  186.0 2.5 convert_reduce_fusion
  188.5 2.6 convolution_convert_fusion.refs_2_
  191.1 2.6 fusion.36.refs_0_
  193.7 72.9 %chain_scatter2.1 = (f32[128,1024]{1,0:T(8,128)S(1)}, f32[1024,512]{1,0:T(8,128)S(1)}, f32[512,1024]{1,0:T(8,128)S(1)}) custom-call(f32[512,1024]{1,0:T(8,128)} %fusion.36.refs_0_, bf16[1024,1024]{1,0:T(8,128)(2,1)} %convolution_convert_fusion.1.refs_1_, bf16[1024,1024]{1,0:T(8,128)(2,1)} %convolution_convert_fusion.refs_2_), custom_call_target="tpu_custom_call" | custom-call | bytes 62914560 | tf_op jit(solution)/shard_map/chain_scatter2/pallas_call | solution.py:499
  267.7 1.6 convert_reduce_fusion.3
  269.3 20.6 %chain_gather0.7 = bf16[512,1024]{1,0:T(8,128)(2,1)S(1)} custom-call(bf16[128,1024]{1,0:T(8,128)(2,1)S(1)} %get-tuple-element.92.refs_0_), custom_call_target="tpu_custom_call" | custom-call | bytes 62914560 | tf_op jit(solution)/shard_map/chain_gather0/pallas_call | solution.py:499
  297.4 2.2 convolution_convert_fusion.2.refs_1_
  299.5 2.4 fusion.18.refs_0_
  302.6 2.5 collective-permute-start.5
  305.1 2.5 collective-permute-start.6
  308.4 1.4 copy-done.4
  309.8 51.1 %chain_scatter3.1 = (f32[128,1024]{1,0:T(8,128)S(1)}, f32[512,768]{1,0:T(8,128)S(1)}, f32[512,256]{1,0:T(8,128)S(1)}, f32[8,1024]{1,0:T(8,128)S(1)}) custom-call(f32[512,1024]{1,0:T(8,128)} %fusion.18.refs_0_, bf16[1024,768]{1,0:T(8,128)(2,1)S(1)} %copy-done.4, bf16[1024,256]{1,0:T(8,128)(2,1)S(1)} %convolution_convert_fusion.3.refs_2_, ...), custom_call_target="tpu_custom_call" | custom-call | bytes 62914560 | tf_op jit(solution)/shard_map/chain_scatter3/pallas_call | solution.py:499
  362.8 2.1 collective-permute-start.10
  367.4 1.9 collective-permute-done.9
  369.3 8.3 %collective-permute-done.10 = bf16[128,512]{1,0:T(8,128)(2,1)S(1)} collective-permute-done((bf16[128,512]{1,0:T(8,128)(2,1)S(1)}, bf16[128,512]{1,0:T(8,128)(2,1)S(1)}, u32[]{:S(2)}, u32[]{:S(2)}) %collective-permute-start.10) | collective-permute-done | bytes 131104 | tf_op jit(solution)/shard_map/ppermute | solution.py:555
  (151 shorter events, 34.7 us)
Async XLA Ops:
  7.2 16.5 %copy-start.28 = (f32[512]{0:T(512)S(1)}, f32[512]{0:T(512)}, u32[]{:S(2)}) copy-start(f32[512]{0:T(512)} %param.28) | copy-start | bytes 6148
  7.2 16.5 %copy-start.27 = (f32[512]{0:T(512)S(1)}, f32[512]{0:T(512)}, u32[]{:S(2)}) copy-start(f32[512]{0:T(512)} %param.27) | copy-start | bytes 6148
  7.2 16.5 %copy-start.26 = (f32[512]{0:T(512)S(1)}, f32[512]{0:T(512)}, u32[]{:S(2)}) copy-start(f32[512]{0:T(512)} %param.26) | copy-start | bytes 6148
  7.2 16.5 %copy-start.25 = (f32[512]{0:T(512)S(1)}, f32[512]{0:T(512)}, u32[]{:S(2)}) copy-start(f32[512]{0:T(512)} %param.22) | copy-start | bytes 6148
  7.2 16.5 %copy-start.24 = (f32[512]{0:T(512)S(1)}, f32[512]{0:T(512)}, u32[]{:S(2)}) copy-start(f32[512]{0:T(512)} %param.21) | copy-start | bytes 6148
  7.2 17.8 %copy-start.21 = (bf16[256,512]{1,0:T(8,128)(2,1)S(1)}, bf16[256,512]{1,0:T(8,128)(2,1)}, u32[]{:S(2)}) copy-start(bf16[256,512]{1,0:T(8,128)(2,1)} %param.19) | copy-start | bytes 786436
  7.3 18.6 %copy-start.16 = (bf16[512,768]{1,0:T(8,128)(2,1)S(1)}, bf16[512,768]{1,0:T(8,128)(2,1)}, u32[]{:S(2)}) copy-start(bf16[512,768]{1,0:T(8,128)(2,1)} %param.17) | copy-start | bytes 2359300
  7.3 19.8 %copy-start.32 = (s32[2]{0:T(128)S(1)}, s32[2]{0:T(128)}, u32[]{:S(2)}) copy-start(s32[2]{0:T(128)} %param.16) | copy-start | bytes 28
  7.3 20.4 %copy-start.22 = (f32[4,128]{1,0:T(4,128)S(1)}, f32[4,128]{1,0:T(4,128)}, u32[]{:S(2)}) copy-start(f32[4,128]{1,0:T(4,128)} %param.18) | copy-start | bytes 6148
  7.3 116.1 %all-gather.3.cloned.1.call-start = ((), (), s32[]{:S(2)}) async-start(), calls=%async_computation | async-start | bytes 3145728 | tf_op jit(solution)/shard_map/all_gather | solution.py:662
  8.4 12.0 %collective-permute-start = (bf16[128,512]{1,0:T(8,128)(2,1)S(1)}, bf16[128,512]{1,0:T(8,128)(2,1)S(1)}, u32[]{:S(2)}, u32[]{:S(2)}) collective-permute-start(bf16[128,512]{1,0:T(8,128)(2,1)S(1)} %get-tuple-element.120), channel_id=1, source_target_pairs={{0,1},{1,3},{2,5},{3,7},{4,0},{5,2},{6,4},{7,6},{8,9},{9,11},{10,1... | collective-permute-start | bytes 393224 | tf_op jit(solution)/shard_map/ppermute | solution.py:541
  11.1 9.3 %collective-permute-start.1 = (bf16[128,512]{1,0:T(8,128)(2,1)S(1)}, bf16[128,512]{1,0:T(8,128)(2,1)S(1)}, u32[]{:S(2)}, u32[]{:S(2)}) collective-permute-start(bf16[128,512]{1,0:T(8,128)(2,1)S(1)} %get-tuple-element.121), channel_id=1, source_target_pairs={{0,0},{1,2},{2,4},{3,6},{4,1},{5,3},{6,5},{7,7},{8,8},{9,10},{10,1... | collective-permute-start | bytes 393224 | tf_op jit(solution)/shard_map/ppermute | solution.py:541
  14.4 6.0 %collective-permute-start.7 = (bf16[128,512]{1,0:T(8,128)(2,1)S(1)}, bf16[128,512]{1,0:T(8,128)(2,1)S(1)}, u32[]{:S(2)}, u32[]{:S(2)}) collective-permute-start(bf16[128,512]{1,0:T(8,128)(2,1)S(1)} %get-tuple-element.112), channel_id=1, source_target_pairs={{0,1},{1,3},{2,5},{3,7},{4,0},{5,2},{6,4},{7,6},{8,9},{9,11},{10,1... | collective-permute-start | bytes 393224 | tf_op jit(solution)/shard_map/ppermute | solution.py:541
  15.8 7.7 %collective-permute-start.8 = (bf16[128,512]{1,0:T(8,128)(2,1)S(1)}, bf16[128,512]{1,0:T(8,128)(2,1)S(1)}, u32[]{:S(2)}, u32[]{:S(2)}) collective-permute-start(bf16[128,512]{1,0:T(8,128)(2,1)S(1)} %get-tuple-element.113), channel_id=1, source_target_pairs={{0,0},{1,2},{2,4},{3,6},{4,1},{5,3},{6,5},{7,7},{8,8},{9,10},{10,1... | collective-permute-start | bytes 393224 | tf_op jit(solution)/shard_map/ppermute | solution.py:541
  23.6 108.5 %all-gather.5.cloned.1.call-start = ((), (), s32[]{:S(2)}) async-start(), calls=%async_computation.1 | async-start | bytes 3145728 | tf_op jit(solution)/shard_map/all_gather | solution.py:663
  23.7 5.5 %collective-permute-start.4 = (f32[6,512]{1,0:T(8,128)S(1)}, f32[6,512]{1,0:T(8,128)S(1)}, u32[]{:S(2)}, u32[]{:S(2)}) collective-permute-start(f32[6,512]{1,0:T(8,128)S(1)} %stack.66), channel_id=1, source_target_pairs={{0,4},{4,0},{1,5},{5,1},{2,6},{6,2},{3,7},{7,3},{8,12},{12,8},{9,1... | collective-permute-start | bytes 36872 | tf_op jit(solution)/shard_map/ppermute | solution.py:622
  25.0 23.0 %collective-permute-start.3 = (bf16[256,512]{1,0:T(8,128)(2,1)S(1)}, bf16[256,512]{1,0:T(8,128)(2,1)S(1)}, u32[]{:S(2)}, u32[]{:S(2)}) collective-permute-start(bf16[256,512]{1,0:T(8,128)(2,1)S(1)} %copy-done.21), channel_id=1, source_target_pairs={{0,4},{4,0},{1,5},{5,1},{2,6},{6,2},{3,7},{7,3},{8,12},{12,8},{9,1... | collective-permute-start | bytes 786440 | tf_op jit(solution)/shard_map/ppermute | solution.py:622
  25.8 39.1 %collective-permute-start.2 = (bf16[512,768]{1,0:T(8,128)(2,1)S(1)}, bf16[512,768]{1,0:T(8,128)(2,1)}, u32[]{:S(2)}, u32[]{:S(2)}) collective-permute-start(bf16[512,768]{1,0:T(8,128)(2,1)S(1)} %copy-done.16), channel_id=1, source_target_pairs={{0,4},{4,0},{1,5},{5,1},{2,6},{6,2},{3,7},{7,3},{8,12},{12,8},{9,1... | collective-permute-start | bytes 2359304 | tf_op jit(solution)/shard_map/ppermute | solution.py:622
  48.0 18.2 %copy-start.5 = (bf16[512,1024]{1,0:T(8,128)(2,1)}, bf16[512,1024]{1,0:T(8,128)(2,1)S(1)}, u32[]{:S(2)}) copy-start(bf16[512,1024]{1,0:T(8,128)(2,1)S(1)} %chain_gather0.4) | copy-start | bytes 3145732
  48.1 26.4 %copy-start.12 = (bf16[256,512]{1,0:T(8,128)(2,1)}, bf16[256,512]{1,0:T(8,128)(2,1)S(1)}, u32[]{:S(2)}) copy-start(bf16[256,512]{1,0:T(8,128)(2,1)S(1)} %get-tuple-element.104) | copy-start | bytes 786436
  48.1 26.4 %copy-start.14 = (bf16[256,512]{1,0:T(8,128)(2,1)}, bf16[256,512]{1,0:T(8,128)(2,1)S(1)}, u32[]{:S(2)}) copy-start(bf16[256,512]{1,0:T(8,128)(2,1)S(1)} %get-tuple-element.105) | copy-start | bytes 786436
  74.5 31.0 %copy-start.10 = (bf16[4,64,512]{2,1,0:T(8,128)(2,1)}, bf16[4,64,512]{2,1,0:T(8,128)(2,1)S(1)}, u32[]{:S(2)}) copy-start(bf16[4,64,512]{2,1,0:T(8,128)(2,1)S(1)} %fusion.17) | copy-start | bytes 786436
  105.4 17.9 %copy-start.31 = (f32[1024]{0:T(1024)S(1)}, f32[1024]{0:T(1024)}, u32[]{:S(2)}) copy-start(f32[1024]{0:T(1024)} %param.24) | copy-start | bytes 12292
  164.1 18.2 %copy-start.33 = (bf16[512,1024]{1,0:T(8,128)(2,1)S(1)}, bf16[512,1024]{1,0:T(8,128)(2,1)}, u32[]{:S(2)}) copy-start(bf16[512,1024]{1,0:T(8,128)(2,1)} %get-tuple-element.97) | copy-start | bytes 3145732
  267.7 22.2 %copy-start.13 = (bf16[256,512]{1,0:T(8,128)(2,1)S(1)}, bf16[256,512]{1,0:T(8,128)(2,1)}, u32[]{:S(2)}) copy-start(bf16[256,512]{1,0:T(8,128)(2,1)} %copy-done.12) | copy-start | bytes 786436
  267.7 22.2 %copy-start.15 = (bf16[256,512]{1,0:T(8,128)(2,1)S(1)}, bf16[256,512]{1,0:T(8,128)(2,1)}, u32[]{:S(2)}) copy-start(bf16[256,512]{1,0:T(8,128)(2,1)} %copy-done.14) | copy-start | bytes 786436
  269.3 21.1 %copy-start.11 = (bf16[4,64,512]{2,1,0:T(8,128)(2,1)S(1)}, bf16[4,64,512]{2,1,0:T(8,128)(2,1)}, u32[]{:S(2)}) copy-start(bf16[4,64,512]{2,1,0:T(8,128)(2,1)} %copy-done.10) | copy-start | bytes 786436
  302.6 64.0 %collective-permute-start.5 = (bf16[128,512]{1,0:T(8,128)(2,1)}, bf16[128,512]{1,0:T(8,128)(2,1)S(1)}, u32[]{:S(2)}, u32[]{:S(2)}) collective-permute-start(bf16[128,512]{1,0:T(8,128)(2,1)} %get-tuple-element.116), channel_id=1, source_target_pairs={{1,0},{3,1},{5,2},{7,3},{0,4},{2,5},{4,6},{6,7},{9,8},{11,9},{13,1... | collective-permute-start | bytes 393224 | tf_op jit(solution)/shard_map/ppermute | solution.py:555
  305.1 61.5 %collective-permute-start.6 = (bf16[128,512]{1,0:T(8,128)(2,1)}, bf16[128,512]{1,0:T(8,128)(2,1)S(1)}, u32[]{:S(2)}, u32[]{:S(2)}) collective-permute-start(bf16[128,512]{1,0:T(8,128)(2,1)} %get-tuple-element.117), channel_id=1, source_target_pairs={{0,0},{2,1},{4,2},{6,3},{1,4},{3,5},{5,6},{7,7},{8,8},{10,9},{12,1... | collective-permute-start | bytes 393224 | tf_op jit(solution)/shard_map/ppermute | solution.py:555
  309.8 52.3 %copy-start.9 = (f32[128,1024]{1,0:T(8,128)S(1)}, f32[128,1024]{1,0:T(8,128)}, u32[]{:S(2)}) copy-start(f32[128,1024]{1,0:T(8,128)} %get-tuple-element.93) | copy-start | bytes 1572868
  362.8 6.5 %collective-permute-start.9 = (bf16[128,512]{1,0:T(8,128)(2,1)S(1)}, bf16[128,512]{1,0:T(8,128)(2,1)S(1)}, u32[]{:S(2)}, u32[]{:S(2)}) collective-permute-start(bf16[128,512]{1,0:T(8,128)(2,1)S(1)} %get-tuple-element.108), channel_id=1, source_target_pairs={{1,0},{3,1},{5,2},{7,3},{0,4},{2,5},{4,6},{6,7},{9,8},{11,9},{13,1... | collective-permute-start | bytes 393224 | tf_op jit(solution)/shard_map/ppermute | solution.py:555
  362.8 14.8 %collective-permute-start.10 = (bf16[128,512]{1,0:T(8,128)(2,1)S(1)}, bf16[128,512]{1,0:T(8,128)(2,1)S(1)}, u32[]{:S(2)}, u32[]{:S(2)}) collective-permute-start(bf16[128,512]{1,0:T(8,128)(2,1)S(1)} %get-tuple-element.109), channel_id=1, source_target_pairs={{0,0},{2,1},{4,2},{6,3},{1,4},{3,5},{5,6},{7,7},{8,8},{10,9},{12,1... | collective-permute-start | bytes 393224 | tf_op jit(solution)/shard_map/ppermute | solution.py:555
  (17 other events, 59.8 us)
Sparse Core Ops, SparseCore 0:
  23.7 47.9 all-gather.2
  73.2 33.6 all-gather.4
